TPU v7x, 128 devices: a whole 4x4x4 slice. The times are simulated.
128 devices in a mesh: dp: 64 (over x, y, z), tensor: 2 (over core).
Axes of the slice: x: 4, y: 4, z: 4, core: 2. Of those that a mesh axis runs over, the one named last changes fastest.
Arguments:
- tokens: bfloat16 [16384, 768], P(('dp', 'tensor')), may hold values from -6 to 6
- gain_attn: float32 [768], replicated, may hold values from 0.5 to 1.5
- rel_table: float32 [32, 12], replicated, may hold values from -5 to 5
- w_qkv: bfloat16 [768, 3, 768], P('dp', None, 'tensor'), may hold values from -0.078125 to 0.078125
- w_o: bfloat16 [768, 768], P(('tensor', 'dp')), may hold values from -5 to 5
- gain_moe: float32 [768], replicated, may hold values from 0.5 to 1.5
- router: float32 [768, 64], replicated, may hold values from -0.15625 to 0.15625
- w_in: bfloat16 [64, 768, 3072], P('dp', None, 'tensor'), may hold values from -0.21875 to 0.21875
- w_out: bfloat16 [64, 3072, 768], P('dp', 'tensor'), may hold values from -5 to 5
- segments: int32 [64, 256], P('dp'), may hold values from 0 to 2, never falling along the last dimension, each value on 1 to 192 neighbouring positions
- offset_buckets: int32 [511], replicated, may hold values from 0 to 31
- expert_ids: int32 [16384, 1], P(('dp', 'tensor')), may hold values from 0 to 63; in each aligned block of 128 rows (0 to 127, 128 to 255, ...) at most 2 rows name the same one
- out_grad: bfloat16 [16384, 768], P(('dp', 'tensor')), may hold values from -6 to 6
Outputs:
- activations: bfloat16 [16384, 768], P(('dp', 'tensor'))
- input_grad: bfloat16 [16384, 768], P(('dp', 'tensor'))
- grad_gain_attn: float32 [768], replicated
- grad_rel_table: float32 [32, 12], replicated
- grad_w_qkv: float32 [768, 3, 768], P('dp', None, 'tensor')
- grad_w_o: float32 [768, 768], P(('tensor', 'dp'))
- grad_gain_moe: float32 [768], replicated
- grad_router: float32 [768, 64], replicated
- grad_w_in: float32 [64, 768, 3072], P('dp', None, 'tensor')
- grad_w_out: float32 [64, 3072, 768], P('dp', 'tensor')
Inputs may be any that keep to these rules, and one draw needn't show every extreme that they name: `segments`: along each row segment numbers never fall, and one segment of each row holds exactly 192 positions. `expert_ids`: among the 128 rows of one device no expert is named more than 2 times, and in every draw some device names some expert exactly 2 times.
All inputs are finite; a program needn't handle non-finite values.
Results may differ from a plain program's by a relative error of at most 0.022.
Values may be sent and summed in bfloat16 or wider, within the bound.
No kernel may reach another device: no remote copies, remote signals or barrier semaphores. Data moves between devices by JAX's collectives and lax.ppermute only.
A program may use at most 128 MiB of HBM per device.

v0:
```python
import jax
import jax.numpy as jnp
from jax import lax
from jax.sharding import PartitionSpec as P

PRECISE = lax.Precision.HIGHEST
EPSILON = 1e-06
MASKED = -1000000000.0


def norm_forward(inputs, gain_vec):
    row_scale = lax.rsqrt(jnp.mean(inputs * inputs, axis=-1, keepdims=True) + EPSILON)
    return (inputs * row_scale * gain_vec, row_scale)


def norm_backward(inputs, row_scale, gain_vec, grad_rows):
    inner_grad = grad_rows * gain_vec
    gain_part = jnp.sum(grad_rows * inputs * row_scale, axis=0)
    spread = jnp.mean(inner_grad * inputs, axis=-1, keepdims=True)
    back_rows = row_scale * inner_grad - row_scale * row_scale * row_scale * inputs * spread
    return (back_rows, gain_part)


def per_device(
    tokens,
    gain_attn,
    rel_table,
    w_qkv,
    w_o,
    gain_moe,
    router,
    w_in,
    w_out,
    segments,
    offset_buckets,
    expert_ids,
    out_grad,
):
    tok_rows, model_width = tokens.shape
    local_cols = w_qkv.shape[2]
    bucket_count = rel_table.shape[0]
    head_size = model_width // rel_table.shape[1]
    local_heads = local_cols // head_size
    seq_len = segments.shape[1]
    tensor_size = lax.axis_size("tensor")
    experts = lax.axis_size("dp") * w_in.shape[0]
    capacity = max(2, 5 * tok_rows // (4 * experts))
    block_rows = min(512, seq_len)
    block_count = seq_len // block_rows
    span = seq_len + block_rows
    tensor_index = lax.axis_index("tensor")
    tokens_f = tokens.astype(jnp.float32)
    normed_one, scale_one = norm_forward(tokens_f, gain_attn)
    first_rows = normed_one.astype(jnp.bfloat16)
    first_all = lax.all_gather(first_rows, "tensor", axis=0, tiled=True)
    qkv_full, wo_full = (
        lax.all_gather(w_qkv, "dp", axis=0, tiled=True),
        lax.all_gather(w_o, "dp", axis=0, tiled=True),
    )
    flat_qkv = qkv_full.reshape(model_width, 3 * local_cols)
    qkv_rows = jnp.dot(first_all, flat_qkv, preferred_element_type=jnp.float32).astype(jnp.bfloat16)
    qkv_rows = qkv_rows.reshape(seq_len, 3, local_heads, head_size)
    query_rows = qkv_rows[:, 0]
    key_rows = qkv_rows[:, 1]
    values = qkv_rows[:, 2]
    table_local = lax.dynamic_slice_in_dim(rel_table, tensor_index * local_heads, local_heads, 1)
    bucket_range = jnp.arange(bucket_count, dtype=jnp.int32)
    bucket_hits = (offset_buckets[:, None] == bucket_range[None, :]).astype(jnp.float32)
    offset_bias = jnp.einsum("bh,rb->hr", table_local, bucket_hits, precision=PRECISE)
    offset_padded = jnp.pad(offset_bias, ((0, 0), (0, 1)))
    seg_row = segments[0]

    def block_bias():
        tiled = jnp.tile(offset_padded, (1, block_rows))
        skewed = tiled[:, block_rows - 1 : block_rows - 1 + block_rows * (span - 1)]
        return skewed.reshape(local_heads, block_rows, span - 1)[:, :, :seq_len]

    def diagonal_sums(block_grad):
        widened = jnp.pad(block_grad, ((0, 0), (0, 0), (0, block_rows - 1)))
        flat = widened.reshape(local_heads, block_rows * (span - 1))
        flat = jnp.pad(flat, ((0, 0), (block_rows - 1, 1)))
        return jnp.sum(flat.reshape(local_heads, block_rows, span), axis=1)

    def block_scores():
        scores = (
            jnp.einsum("ihd,jhd->hij", query_rows, key_rows, preferred_element_type=jnp.float32)
            + block_bias()
        )
        same_doc = seg_row[:, None] == seg_row[None, :]
        return (jnp.where(same_doc[None], scores, MASKED), query_rows)

    def attend_block(number):
        scores, block_query = block_scores()
        row_top = jnp.max(scores, axis=-1, keepdims=True)
        shifted = jnp.exp(scores - row_top)
        row_total = jnp.sum(shifted, axis=-1, keepdims=True)
        attn_probs = (shifted / row_total).astype(jnp.bfloat16)
        block_context = jnp.einsum(
            "hij,jhd->ihd", attn_probs, values, preferred_element_type=jnp.float32
        )
        log_total = (row_top + jnp.log(row_total))[..., 0]
        return (block_context.reshape(block_rows, local_cols).astype(jnp.bfloat16), log_total)

    context, log_totals = lax.map(attend_block, jnp.arange(block_count, dtype=jnp.int32))
    context = context.reshape(seq_len, local_cols)
    attn_out = lax.psum_scatter(
        jnp.dot(context, wo_full, preferred_element_type=jnp.float32).astype(jnp.bfloat16),
        "tensor",
        scatter_dimension=0,
        tiled=True,
    ).astype(jnp.float32)
    mid_rows = tokens_f + attn_out
    second_rows, scale_two = norm_forward(mid_rows, gain_moe)
    logits = jnp.dot(second_rows, router, precision=PRECISE)
    router_probs = jax.nn.softmax(logits, axis=-1)
    expert_index = expert_ids[:, 0]
    expert_hits = expert_index[:, None] == jnp.arange(experts, dtype=jnp.int32)[None, :]
    hits_float = expert_hits.astype(jnp.float32)
    gate_value = jnp.sum(router_probs * hits_float, axis=-1)
    second_low = second_rows.astype(jnp.bfloat16)
    hit_counts = jnp.cumsum(expert_hits.astype(jnp.int32), axis=0)
    slot_index = jnp.sum((hit_counts - 1) * expert_hits.astype(jnp.int32), axis=-1)
    slot_target = expert_index * capacity + slot_index
    slot_table = jnp.arange(experts * capacity, dtype=jnp.int32)[:, None] == slot_target[None, :]
    slot_low = slot_table.astype(jnp.bfloat16)
    slot_float = slot_table.astype(jnp.float32)
    outgoing = jnp.dot(slot_low, second_low, preferred_element_type=jnp.float32).astype(
        jnp.bfloat16
    )
    doubled = jnp.broadcast_to(
        outgoing.reshape(experts, 1, capacity, model_width),
        (experts, tensor_size, capacity, model_width),
    )
    arrived = lax.all_to_all(
        doubled.reshape(experts * tensor_size * capacity, model_width),
        ("dp", "tensor"),
        split_axis=0,
        concat_axis=0,
        tiled=True,
    )
    first_weight = w_in[0]
    second_weight = w_out[0]
    pre_act = jnp.dot(arrived, first_weight, preferred_element_type=jnp.float32)
    activated, gelu_back = jax.vjp(lambda inputs: jax.nn.gelu(inputs, approximate=False), pre_act)
    hidden = activated.astype(jnp.bfloat16)
    partial_out = jnp.dot(hidden, second_weight, preferred_element_type=jnp.float32)
    returned = lax.all_to_all(
        partial_out.astype(jnp.bfloat16), ("dp", "tensor"), split_axis=0, concat_axis=0, tiled=True
    ).astype(partial_out.dtype)
    slot_out = jnp.sum(
        returned.reshape(experts, tensor_size, capacity, model_width), axis=1
    ).reshape(experts * capacity, model_width)
    expert_out = jnp.einsum("st,sd->td", slot_float, slot_out, precision=PRECISE)
    activations = (mid_rows + gate_value[:, None] * expert_out).astype(jnp.bfloat16)
    grad_rows = out_grad.astype(jnp.float32)
    grad_gate = jnp.sum(grad_rows * expert_out, axis=-1)
    grad_expert = (gate_value[:, None] * grad_rows).astype(jnp.bfloat16)
    grad_slots = jnp.dot(slot_low, grad_expert, preferred_element_type=jnp.float32).astype(
        jnp.bfloat16
    )
    grad_doubled = jnp.broadcast_to(
        grad_slots.reshape(experts, 1, capacity, model_width),
        (experts, tensor_size, capacity, model_width),
    )
    grad_arrived = lax.all_to_all(
        grad_doubled.reshape(experts * tensor_size * capacity, model_width),
        ("dp", "tensor"),
        split_axis=0,
        concat_axis=0,
        tiled=True,
    )
    grad_hidden = jnp.einsum(
        "rd,fd->rf", grad_arrived, second_weight, preferred_element_type=jnp.float32
    )
    grad_w_out = jnp.einsum("rf,rd->fd", hidden, grad_arrived, preferred_element_type=jnp.float32)
    grad_pre = gelu_back(grad_hidden)[0].astype(jnp.bfloat16)
    grad_w_in = jnp.einsum("rd,rf->df", arrived, grad_pre, preferred_element_type=jnp.float32)
    grad_dispatched = jnp.einsum(
        "rf,df->rd", grad_pre, first_weight, preferred_element_type=jnp.float32
    )
    grad_returned = lax.all_to_all(
        grad_dispatched.astype(jnp.bfloat16),
        ("dp", "tensor"),
        split_axis=0,
        concat_axis=0,
        tiled=True,
    ).astype(grad_dispatched.dtype)
    grad_slot_rows = jnp.sum(
        grad_returned.reshape(experts, tensor_size, capacity, model_width), axis=1
    ).reshape(experts * capacity, model_width)
    grad_second = jnp.einsum("st,sd->td", slot_float, grad_slot_rows, precision=PRECISE)
    grad_logits = (grad_gate * gate_value)[:, None] * (hits_float - router_probs)
    grad_router = jnp.einsum("td,te->de", second_rows, grad_logits, precision=PRECISE)
    grad_second = grad_second + jnp.einsum("te,de->td", grad_logits, router, precision=PRECISE)
    grad_mid_norm, grad_gain_two = norm_backward(mid_rows, scale_two, gain_moe, grad_second)
    grad_mid = grad_rows + grad_mid_norm
    grad_attn = grad_mid.astype(jnp.bfloat16)
    grad_attn_all = lax.all_gather(grad_attn, "tensor", axis=0, tiled=True)
    grad_w_o = jnp.einsum("sc,sd->cd", context, grad_attn_all, preferred_element_type=jnp.float32)
    grad_context = jnp.einsum(
        "sd,cd->sc", grad_attn_all, wo_full, preferred_element_type=jnp.float32
    ).astype(jnp.bfloat16)
    grad_context = grad_context.reshape(seq_len, local_heads, head_size)

    def back_block(state_carry, number):
        grad_keys, grad_values, grad_offsets = state_carry
        scores, block_query = block_scores()
        attn_probs = jnp.exp(scores - log_totals[number][..., None])
        grad_probs = jnp.einsum(
            "ihd,jhd->hij", grad_context, values, preferred_element_type=jnp.float32
        )
        inner_sum = jnp.sum(attn_probs * grad_probs, axis=-1, keepdims=True)
        grad_scores = (attn_probs * (grad_probs - inner_sum)).astype(jnp.bfloat16)
        grad_query = jnp.einsum(
            "hij,jhd->ihd", grad_scores, key_rows, preferred_element_type=jnp.float32
        )
        grad_keys = grad_keys + jnp.einsum(
            "hij,ihd->jhd", grad_scores, block_query, preferred_element_type=jnp.float32
        )
        grad_values = grad_values + jnp.einsum(
            "hij,ihd->jhd",
            attn_probs.astype(jnp.bfloat16),
            grad_context,
            preferred_element_type=jnp.float32,
        )
        sums_here = diagonal_sums(grad_scores.astype(jnp.float32))
        current = grad_offsets
        grad_offsets = current + sums_here
        return ((grad_keys, grad_values, grad_offsets), grad_query)

    zero_rows = jnp.zeros((seq_len, local_heads, head_size), jnp.float32)
    zero_offsets = jnp.zeros((local_heads, 2 * seq_len), jnp.float32)
    (grad_keys, grad_values, grad_offsets), grad_query = lax.scan(
        back_block, (zero_rows, zero_rows, zero_offsets), jnp.arange(block_count, dtype=jnp.int32)
    )
    grad_table = jnp.einsum(
        "hr,rb->hb", grad_offsets[:, : 2 * seq_len - 1], bucket_hits, precision=PRECISE
    )
    grad_qkv = jnp.stack(
        [
            grad_query.reshape(seq_len, local_cols),
            grad_keys.reshape(seq_len, local_cols),
            grad_values.reshape(seq_len, local_cols),
        ],
        axis=1,
    )
    grad_qkv = grad_qkv.astype(jnp.bfloat16).reshape(seq_len, 3 * local_cols)
    grad_w_qkv = jnp.einsum(
        "sd,sk->dk", first_all, grad_qkv, preferred_element_type=jnp.float32
    ).reshape(model_width, 3, local_cols)
    grad_first_all = jnp.einsum("sk,dk->sd", grad_qkv, flat_qkv, preferred_element_type=jnp.float32)
    grad_first = lax.psum_scatter(
        grad_first_all.astype(jnp.bfloat16), "tensor", scatter_dimension=0, tiled=True
    ).astype(jnp.float32)
    grad_input_norm, grad_gain_one = norm_backward(tokens_f, scale_one, gain_attn, grad_first)
    input_grad = (grad_mid + grad_input_norm).astype(jnp.bfloat16)
    grad_qkv_shard, grad_o_shard = (
        lax.psum_scatter(grad_w_qkv, "dp", scatter_dimension=0, tiled=True),
        lax.psum_scatter(grad_w_o, "dp", scatter_dimension=0, tiled=True),
    )
    table_full = lax.dynamic_update_slice_in_dim(
        jnp.zeros((bucket_count, rel_table.shape[1]), jnp.float32),
        grad_table.T,
        tensor_index * local_heads,
        1,
    )
    gain_one_sum, gain_two_sum, table_sum, router_sum = lax.psum(
        (grad_gain_one, grad_gain_two, table_full, grad_router), ("dp", "tensor")
    )
    return (
        activations,
        input_grad,
        gain_one_sum,
        table_sum,
        grad_qkv_shard,
        grad_o_shard,
        gain_two_sum,
        router_sum,
        grad_w_in[None],
        grad_w_out[None],
    )


def solution(mesh):
    in_specs = (
        P(("dp", "tensor"), None),
        P(),
        P(),
        P("dp", None, "tensor"),
        P(("tensor", "dp"), None),
        P(),
        P(),
        P("dp", None, "tensor"),
        P("dp", "tensor", None),
        P("dp", None),
        P(),
        P(("dp", "tensor"), None),
        P(("dp", "tensor"), None),
    )
    out_specs = (
        P(("dp", "tensor"), None),
        P(("dp", "tensor"), None),
        P(),
        P(),
        P("dp", None, "tensor"),
        P(("tensor", "dp"), None),
        P(),
        P(),
        P("dp", None, "tensor"),
        P("dp", "tensor", None),
    )
    return jax.shard_map(
        per_device, mesh=mesh, in_specs=in_specs, out_specs=out_specs, check_vma=False
    )
```

profile of v0, /device:TPU:1, one launch (start us, length us, event | category | flops | bytes accessed | tf_op | source)
XLA Modules:
  0.0 860.3 jit_solution(4437609448812365732)
XLA Ops:
  9.4 1.9 copy.86
  11.3 3.2 slice.33
  14.5 6.4 reshape.194
  20.9 2.7 slice.34
  23.6 3.0 copy.84
  26.7 166.5 %all-gather = bf16[64,6,768]{2,1,0:T(8,128)(2,1)} all-gather(bf16[1,6,768]{2,1,0:T(8,128)(2,1)S(1)} %bitcast.139), channel_id=1, replica_groups=mesh['dp'=64,'tensor'=2] {'dp'}, dimensions={0}, use_global_device_ids=true | all-gather | bytes 599040 | tf_op jit(solution)/shard_map/all_gather | solution.py:58
  195.3 29.5 %all_gather.12 = bf16[256,768]{1,0:T(8,128)(2,1)} all-gather(bf16[128,768]{1,0:T(8,128)(2,1)S(1)} %fusion.39), channel_id=1, replica_groups=mesh['dp'=64,'tensor'=2] {'tensor'}, dimensions={0}, use_global_device_ids=true | all-gather | bytes 589824 | tf_op jit(solution)/shard_map/all_gather | solution.py:55
  224.9 5.3 copy.58
  230.2 3.1 convolution_convert_fusion
  233.3 2.1 copy.59
  235.5 2.1 fusion.85
  247.0 1.9 convolution_convert_fusion.3
  252.4 9.9 %all-to-all-start = ((bf16[128,2,768]{2,1,0:T(2,128)(2,1)}), bf16[128,2,768]{2,1,0:T(2,128)(2,1)}, u32[]{:S(2)}, u32[]{:S(2)}) async-start(bf16[128,2,768]{2,1,0:T(2,128)(2,1)} %bitcast.127), calls=%async_computation.1 | async-start | bytes 786432 | tf_op jit(solution)/shard_map/all_to_all | solution.py:134
  269.2 5.0 all-to-all-done
  276.0 5.6 all-to-all-start.2
  281.6 1.9 all_to_all.30
  283.5 6.1 multiply_convert_fusion.1
  289.6 4.1 all-to-all-done.2
  293.7 1.9 all_to_all.35
  295.6 3.8 add_convert_fusion
  301.8 2.0 all_to_all.36
  303.8 5.8 all-to-all-start.3
  309.7 2.5 fusion.22
  313.1 4.2 convolution_bitcast_fusion.1
  317.3 3.0 convolution_bitcast_fusion
  321.9 8.1 all-to-all-start.1
  331.5 10.8 %all-to-all-done.1 = bf16[128,2,768]{2,1,0:T(2,128)(2,1)S(1)} async-done(((bf16[128,2,768]{2,1,0:T(2,128)(2,1)}), bf16[128,2,768]{2,1,0:T(2,128)(2,1)S(1)}, u32[]{:S(2)}, u32[]{:S(2)}) %all-to-all-start.1) | async-done | bytes 393248 | tf_op jit(solution)/shard_map/all_to_all | solution.py:147
  346.3 3.0 all_gather.15
  357.3 2.9 fusion.18
  360.4 155.9 %fusion = f32[8,768]{1,0:T(8,128)} fusion(f32[384,768]{1,0:T(8,128)S(1)} %fusion.87), kind=kCustom, calls=%all-reduce-scatter | all-reduce-scatter fusion | flops 393217 | bytes 1204736
  517.9 1.9 collective-permute-start.14
  523.6 1.9 collective-permute-start.11
  525.6 4.0 reshape.214
  529.6 3.0 reshape.198
  536.4 3.5 fusion.29
  540.0 2.6 pad_convert_fusion
  545.2 10.1 %collective-permute-start.9 = (f32[8,768]{1,0:T(8,128)}, f32[8,768]{1,0:T(8,128)S(1)}, u32[]{:S(2)}, u32[]{:S(2)}) collective-permute-start(f32[8,768]{1,0:T(8,128)} %fusion), channel_id=1, source_target_pairs={{0,20},{2,22},{4,24},{6,26},{8,28},{10,30},{12,32},{14,34},{16,36}... | collective-permute-start | bytes 73736
  558.5 4.4 collective-permute-start.6
  562.9 2.2 collective-permute-start.5
  565.1 3.8 bitcast_reduce_fusion
  569.0 2.6 collective-permute-start.4
  571.6 2.5 collective-permute-start.3
  574.1 5.3 collective-permute-start.2
  581.3 3.1 collective-permute-start
  584.9 24.3 %concatenate = f32[134,768]{1,0:T(8,128)} concatenate(f32[6,768]{1,0:T(8,128)} %copy-done.24, f32[8,768]{1,0:T(8,128)} %collective-permute-done.14, f32[8,768]{1,0:T(8,128)} %collective-permute-done.13, f32[8,768]{1,0:T(8,128)} %collective-permute-done.12, f32[8,768]{1,0:T(8,128)} %collective-permute-done.11, f32[8,768]{1,0:T(8,128)S(1)} %collective-permute-done.10, ...), dimensions={0} | concatenate | bytes 823296
  611.8 96.0 %all-reduce.6 = (f32[768]{0:T(1024)}, f32[32,12]{0,1:T(8,128)}, f32[768]{0:T(1024)}) all-reduce(f32[768]{0:T(1024)S(1)} %get-tuple-element.102, f32[32,12]{0,1:T(8,128)S(1)} %dynamic_update_slice.12, f32[768]{0:T(1024)} %get-tuple-element.100), channel_id=1, replica_groups=mesh['dp'=64,'tensor'=2] {'dp','tensor'}, use_global_device_ids=true, to_apply=%region_18.19 | all-reduce | flops 1920 | bytes 15360 | tf_op jit(solution)/shard_map/psum | solution.py:267
  707.8 2.2 fusion.34
  711.5 140.2 %all-reduce.10.cloned.1.call-done = f32[768,64]{0,1:T(8,128)} async-done(((f32[768,64]{0,1:T(8,128)}), f32[768,64]{0,1:T(8,128)}) %all-reduce.10.cloned.1.call-update) | async-done | bytes 196624 | tf_op jit(solution)/shard_map/psum | solution.py:267
  (207 shorter events, 66.0 us)
Async XLA Ops:
  7.2 276.3 %copy-start = (bf16[1,768,1536]{2,1,0:T(8,128)(2,1)S(1)}, bf16[1,768,1536]{2,1,0:T(8,128)(2,1)}, u32[]{:S(2)}) copy-start(bf16[1,768,1536]{2,1,0:T(8,128)(2,1)} %param.20) | copy-start | bytes 7077892
  7.2 217.7 %all-gather.3.cloned.1.call-start = ((), (), s32[]{:S(2)}) async-start(), calls=%async_computation.6 | async-start | bytes 2396160 | tf_op jit(solution)/shard_map/all_gather | solution.py:57
  7.9 236.8 %reduce-scatter.6.cloned.1.call-start = ((), (), s32[]{:S(2)}) async-start(), calls=%async_computation.7 | async-start | bytes 589824 | tf_op jit(solution)/shard_map/reduce_scatter | solution.py:106
  26.7 167.8 %copy-start.4 = (bf16[128,768]{1,0:T(8,128)(2,1)S(1)}, bf16[128,768]{1,0:T(8,128)(2,1)}, u32[]{:S(2)}) copy-start(bf16[128,768]{1,0:T(8,128)(2,1)} %param.13) | copy-start | bytes 589828
  26.7 168.5 %copy-start.23 = (f32[768]{0:T(1024)S(1)}, f32[768]{0:T(1024)}, u32[]{:S(2)}) copy-start(f32[768]{0:T(1024)} %param.14) | copy-start | bytes 9220
  26.7 198.1 %copy-start.44 = (s32[1,256]{1,0:T(1,128)S(1)}, s32[1,256]{1,0:T(1,128)}, u32[]{:S(2)}) copy-start(s32[1,256]{1,0:T(1,128)} %param.22) | copy-start | bytes 3076
  195.2 35.0 %copy-start.41 = (f32[128]{0:T(128)}, f32[128]{0:T(128)S(1)}, u32[]{:S(2)}) copy-start(f32[128]{0:T(128)S(1)} %get-tuple-element.114) | copy-start | bytes 1540
  239.4 7.6 copy-start.22
  244.7 17.6 %copy-start.5 = (bf16[128,768]{1,0:T(8,128)(2,1)S(1)}, bf16[128,768]{1,0:T(8,128)(2,1)}, u32[]{:S(2)}) copy-start(bf16[128,768]{1,0:T(8,128)(2,1)} %reduce-scatter.6.cloned.1.call-done) | copy-start | bytes 589828
  245.9 20.0 %copy-start.11 = (bf16[128,768]{1,0:T(8,128)(2,1)S(1)}, bf16[128,768]{1,0:T(8,128)(2,1)}, u32[]{:S(2)}) copy-start(bf16[128,768]{1,0:T(8,128)(2,1)} %param.25) | copy-start | bytes 589828
  252.4 21.7 %all-to-all-start = ((bf16[128,2,768]{2,1,0:T(2,128)(2,1)}), bf16[128,2,768]{2,1,0:T(2,128)(2,1)}, u32[]{:S(2)}, u32[]{:S(2)}) async-start(bf16[128,2,768]{2,1,0:T(2,128)(2,1)} %bitcast.127), calls=%async_computation.1 | async-start | bytes 786432 | tf_op jit(solution)/shard_map/all_to_all | solution.py:134
  276.0 17.7 %all-to-all-start.2 = ((bf16[128,2,768]{2,1,0:T(2,128)(2,1)}), bf16[128,2,768]{2,1,0:T(2,128)(2,1)}, u32[]{:S(2)}, u32[]{:S(2)}) async-start(bf16[128,2,768]{2,1,0:T(2,128)(2,1)} %bitcast.128), calls=%async_computation.3 | async-start | bytes 786432 | tf_op jit(solution)/shard_map/all_to_all | solution.py:165
  301.8 7.8 copy-start.12
  303.8 18.1 %all-to-all-start.3 = ((bf16[128,2,768]{2,1,0:T(2,128)(2,1)}), bf16[128,2,768]{2,1,0:T(2,128)(2,1)S(1)}, u32[]{:S(2)}, u32[]{:S(2)}) async-start(bf16[128,2,768]{2,1,0:T(2,128)(2,1)} %all_to_all.36), calls=%async_computation.4 | async-start | bytes 786432 | tf_op jit(solution)/shard_map/all_to_all | solution.py:181
  320.3 10.8 %copy-start.40 = (s32[128]{0:T(128)S(1)}, s32[128]{0:T(128)}, u32[]{:S(2)}) copy-start(s32[128]{0:T(128)} %multiply_add_fusion) | copy-start | bytes 1540
  321.9 20.4 %all-to-all-start.1 = ((bf16[128,2,768]{2,1,0:T(2,128)(2,1)}), bf16[128,2,768]{2,1,0:T(2,128)(2,1)S(1)}, u32[]{:S(2)}, u32[]{:S(2)}) async-start(bf16[128,2,768]{2,1,0:T(2,128)(2,1)} %all_to_all.31), calls=%async_computation.2 | async-start | bytes 786432 | tf_op jit(solution)/shard_map/all_to_all | solution.py:147
  330.0 280.6 %reduce-scatter.8.cloned.1.call-start = ((), (), s32[]{:S(2)}) async-start(), calls=%async_computation.8 | async-start | bytes 589824 | tf_op jit(solution)/shard_map/reduce_scatter | solution.py:252
  331.1 13.1 %copy-start.43 = (f32[128]{0:T(128)S(1)}, f32[128]{0:T(128)}, u32[]{:S(2)}) copy-start(f32[128]{0:T(128)} %copy-done.42) | copy-start | bytes 1540
  331.1 13.1 %copy-start.16 = (f32[128,64]{0,1:T(8,128)S(1)}, f32[128,64]{0,1:T(8,128)}, u32[]{:S(2)}) copy-start(f32[128,64]{0,1:T(8,128)} %copy-done.15) | copy-start | bytes 98308
  331.1 13.1 %copy-start.18 = (f32[768,64]{0,1:T(8,128)S(1)}, f32[768,64]{0,1:T(8,128)}, u32[]{:S(2)}) copy-start(f32[768,64]{0,1:T(8,128)} %param.19) | copy-start | bytes 589828
  331.1 13.1 %copy-start.27 = (f32[128]{0:T(128)S(1)}, f32[128]{0:T(128)}, u32[]{:S(2)}) copy-start(f32[128]{0:T(128)} %copy-done.26) | copy-start | bytes 1540
  331.1 13.1 %copy-start.31 = (s32[128,1]{0,1:T(1,128)S(1)}, s32[128,1]{0,1:T(1,128)}, u32[]{:S(2)}) copy-start(s32[128,1]{0,1:T(1,128)} %param.24) | copy-start | bytes 1540
  331.1 13.1 %copy-start.34 = (f32[128]{0:T(128)S(1)}, f32[128]{0:T(128)}, u32[]{:S(2)}) copy-start(f32[128]{0:T(128)} %copy-done.33) | copy-start | bytes 1540
  331.1 13.1 %copy-start.38 = (f32[128]{0:T(128)S(1)}, f32[128]{0:T(128)}, u32[]{:S(2)}) copy-start(f32[128]{0:T(128)} %copy-done.37) | copy-start | bytes 1540
  345.5 5.9 copy-start.7
  346.1 5.3 copy-start.3
  360.3 349.6 %all-reduce.12.cloned.1.call-start = ((), (), s32[]{:S(2)}) async-start(), calls=%async_computation.10 | async-start | bytes 7077888
  517.9 27.2 %collective-permute-start.14 = (f32[8,768]{1,0:T(8,128)}, f32[8,768]{1,0:T(8,128)}, u32[]{:S(2)}, u32[]{:S(2)}) collective-permute-start(f32[8,768]{1,0:T(8,128)} %fusion), channel_id=1, source_target_pairs={{0,30},{2,32},{4,34},{6,36},{8,38},{10,40},{12,42},{14,44},{16,46}... | collective-permute-start | bytes 73736
  519.8 35.5 %collective-permute-start.13 = (f32[8,768]{1,0:T(8,128)}, f32[8,768]{1,0:T(8,128)}, u32[]{:S(2)}, u32[]{:S(2)}) collective-permute-start(f32[8,768]{1,0:T(8,128)} %fusion), channel_id=1, source_target_pairs={{0,28},{2,30},{4,32},{6,34},{8,36},{10,38},{12,40},{14,42},{16,44}... | collective-permute-start | bytes 73736
  521.7 34.9 %collective-permute-start.12 = (f32[8,768]{1,0:T(8,128)}, f32[8,768]{1,0:T(8,128)}, u32[]{:S(2)}, u32[]{:S(2)}) collective-permute-start(f32[8,768]{1,0:T(8,128)} %fusion), channel_id=1, source_target_pairs={{0,26},{2,28},{4,30},{6,32},{8,34},{10,36},{12,38},{14,40},{16,42}... | collective-permute-start | bytes 73736
  523.6 34.9 %collective-permute-start.11 = (f32[8,768]{1,0:T(8,128)}, f32[8,768]{1,0:T(8,128)}, u32[]{:S(2)}, u32[]{:S(2)}) collective-permute-start(f32[8,768]{1,0:T(8,128)} %fusion), channel_id=1, source_target_pairs={{0,24},{2,26},{4,28},{6,30},{8,32},{10,34},{12,36},{14,38},{16,40}... | collective-permute-start | bytes 73736
  534.9 7.8 collective-permute-start.15
  540.0 311.8 %all-reduce.10.cloned.1.call-start = ((), (), s32[]{:S(2)}) async-start(), calls=%async_computation.9 | async-start | bytes 393216 | tf_op jit(solution)/shard_map/psum | solution.py:267
  542.7 26.3 %copy-start.24 = (f32[6,768]{1,0:T(8,128)}, f32[6,768]{1,0:T(8,128)S(1)}, u32[]{:S(2)}) copy-start(f32[6,768]{1,0:T(8,128)S(1)} %collective-permute-done.15) | copy-start | bytes 55300
  542.7 20.2 %collective-permute-start.10 = (f32[8,768]{1,0:T(8,128)}, f32[8,768]{1,0:T(8,128)S(1)}, u32[]{:S(2)}, u32[]{:S(2)}) collective-permute-start(f32[8,768]{1,0:T(8,128)} %fusion), channel_id=1, source_target_pairs={{0,22},{2,24},{4,26},{6,28},{8,30},{10,32},{12,34},{14,36},{16,38}... | collective-permute-start | bytes 73736
  545.2 23.8 %collective-permute-start.9 = (f32[8,768]{1,0:T(8,128)}, f32[8,768]{1,0:T(8,128)S(1)}, u32[]{:S(2)}, u32[]{:S(2)}) collective-permute-start(f32[8,768]{1,0:T(8,128)} %fusion), channel_id=1, source_target_pairs={{0,20},{2,22},{4,24},{6,26},{8,28},{10,30},{12,32},{14,34},{16,36}... | collective-permute-start | bytes 73736
  555.3 16.3 %collective-permute-start.8 = (f32[8,768]{1,0:T(8,128)}, f32[8,768]{1,0:T(8,128)S(1)}, u32[]{:S(2)}, u32[]{:S(2)}) collective-permute-start(f32[8,768]{1,0:T(8,128)} %fusion), channel_id=1, source_target_pairs={{0,18},{2,20},{4,22},{6,24},{8,26},{10,28},{12,30},{14,32},{16,34}... | collective-permute-start | bytes 73736
  556.6 17.5 %collective-permute-start.7 = (f32[8,768]{1,0:T(8,128)}, f32[8,768]{1,0:T(8,128)S(1)}, u32[]{:S(2)}, u32[]{:S(2)}) collective-permute-start(f32[8,768]{1,0:T(8,128)} %fusion), channel_id=1, source_target_pairs={{0,16},{2,18},{4,20},{6,22},{8,24},{10,26},{12,28},{14,30},{16,32}... | collective-permute-start | bytes 73736
  558.5 20.9 %collective-permute-start.6 = (f32[8,768]{1,0:T(8,128)}, f32[8,768]{1,0:T(8,128)S(1)}, u32[]{:S(2)}, u32[]{:S(2)}) collective-permute-start(f32[8,768]{1,0:T(8,128)} %fusion), channel_id=1, source_target_pairs={{0,14},{2,16},{4,18},{6,20},{8,22},{10,24},{12,26},{14,28},{16,30}... | collective-permute-start | bytes 73736
  562.9 18.4 %collective-permute-start.5 = (f32[8,768]{1,0:T(8,128)}, f32[8,768]{1,0:T(8,128)S(1)}, u32[]{:S(2)}, u32[]{:S(2)}) collective-permute-start(f32[8,768]{1,0:T(8,128)} %fusion), channel_id=1, source_target_pairs={{0,12},{2,14},{4,16},{6,18},{8,20},{10,22},{12,24},{14,26},{16,28}... | collective-permute-start | bytes 73736
  565.1 19.3 %copy-start.50 = (s32[511]{0:T(512)S(1)}, s32[511]{0:T(512)}, u32[]{:S(2)}) copy-start(s32[511]{0:T(512)} %param.23) | copy-start | bytes 6136
  569.0 138.8 %copy-start.8 = (f32[128,768]{1,0:T(8,128)S(1)}, f32[128,768]{1,0:T(8,128)}, u32[]{:S(2)}) copy-start(f32[128,768]{1,0:T(8,128)} %copy-done.7) | copy-start | bytes 1179652
  569.0 15.9 %collective-permute-start.4 = (f32[8,768]{1,0:T(8,128)}, f32[8,768]{1,0:T(8,128)S(1)}, u32[]{:S(2)}, u32[]{:S(2)}) collective-permute-start(f32[8,768]{1,0:T(8,128)} %fusion), channel_id=1, source_target_pairs={{0,10},{2,12},{4,14},{6,16},{8,18},{10,20},{12,22},{14,24},{16,26}... | collective-permute-start | bytes 73736
  571.6 13.3 %collective-permute-start.3 = (f32[8,768]{1,0:T(8,128)}, f32[8,768]{1,0:T(8,128)S(1)}, u32[]{:S(2)}, u32[]{:S(2)}) collective-permute-start(f32[8,768]{1,0:T(8,128)} %fusion), channel_id=1, source_target_pairs={{0,8},{2,10},{4,12},{6,14},{8,16},{10,18},{12,20},{14,22},{16,24},... | collective-permute-start | bytes 73736
  574.1 10.8 %collective-permute-start.2 = (f32[8,768]{1,0:T(8,128)}, f32[8,768]{1,0:T(8,128)}, u32[]{:S(2)}, u32[]{:S(2)}) collective-permute-start(f32[8,768]{1,0:T(8,128)} %fusion), channel_id=1, source_target_pairs={{0,6},{2,8},{4,10},{6,12},{8,14},{10,16},{12,18},{14,20},{16,22},{... | collective-permute-start | bytes 73736
  579.4 5.5 collective-permute-start.1
  581.3 3.7 collective-permute-start
  584.9 268.4 %copy-start.1 = (bf16[1,768,1536]{2,1,0:T(8,128)(2,1)S(1)}, bf16[1,768,1536]{2,1,0:T(8,128)(2,1)}, u32[]{:S(2)}) copy-start(bf16[1,768,1536]{2,1,0:T(8,128)(2,1)} %param.20) | copy-start | bytes 7077892
  (28 other events, 64.4 us)
Sparse Core Ops, SparseCore 0:
  10.9 68.3 all-gather.2
  240.7 3.9 reduce-scatter.5
  360.4 6.4 reduce-scatter.7
  540.0 164.1 all-reduce.11
  710.1 141.6 all-reduce.9
where the time goes:
time: 871 us; the launch traced here: 860 us
  blocking collectives  451 us (52%)
  waiting for transfers between devices  164 us (19%)
  local copies, waits for them, and re-layouts  87.1 us (10%)
  starting transfers between devices  75.5 us (9%)
  matrix products  50.1 us (6%)
  other arithmetic  16.4 us (2%)
  between operations  16.4 us (2%)
    all_gather x1, blocking collectives, per_device(): lax.all_gather(w_o, 'dp', axis=0, tiled=True)  166 us
    unnamed x1, blocking collectives  156 us
    psum x1, waiting for transfers between devices, per_device(): lax.psum((grad_gain_one, grad_gain_two, table_full, grad_router), ('dp',...  140 us
    psum x1, blocking collectives, per_device(): lax.psum((grad_gain_one, grad_gain_two, table_full, grad_router), ('dp',...  96 us
    unnamed x115, local copies, waits for them, and re-layouts  45.8 us
    unnamed x17, starting transfers between devices  45.7 us
    all_gather x1, blocking collectives, per_device(): first_all = lax.all_gather(first_rows, 'tensor', axis=0, tiled=True)  29.5 us
  transfers between devices with their start and end apart: 25, of which 7 were waited for; matrix products, arithmetic and copies ran while one was open for 29% of the time, Pallas kernels for 0%

commit v1 on v0

v1 whole, which is shorter than its diff:
```python
import jax
import jax.numpy as jnp
from jax import lax
from jax.sharding import PartitionSpec as P

PRECISE = lax.Precision.HIGHEST
EPSILON = 1e-06
MASKED = -1000000000.0
BF = jnp.bfloat16
F32 = jnp.float32
ALL = ("dp", "tensor")


def swap(rows):
    return lax.ppermute(rows, "tensor", [(0, 1), (1, 0)])


def dot(left, right, dims=((1,), (0,)), precision=None):
    return lax.dot_general(left, right, (dims, ((), ())), precision=precision, preferred_element_type=F32)


def per_device(
    tokens, gain_attn, rel_table, w_qkv, w_o, gain_moe, router, w_in, w_out, segments, offset_buckets, expert_ids, out_grad
):
    rows, width = tokens.shape
    shard, _, cols = w_qkv.shape
    wo_rows = w_o.shape[0]
    buckets, heads_all = rel_table.shape
    head = width // heads_all
    heads = cols // head
    seq = segments.shape[1]
    n_dp = lax.axis_size("dp")
    n_t = lax.axis_size("tensor")
    experts = n_dp
    cap = rows // experts
    t = lax.axis_index("tensor")
    me = lax.axis_index("dp")

    expert_index = expert_ids[:, 0]
    hits = expert_index[:, None] == jnp.arange(experts, dtype=jnp.int32)[None, :]
    counts = jnp.cumsum(hits.astype(jnp.int32), axis=0)
    rank = jnp.sum((counts - 1) * hits.astype(jnp.int32), axis=-1)
    target = expert_index * cap + rank
    slot_hit = jnp.arange(rows, dtype=jnp.int32)[:, None] == target[None, :]
    slot_low = slot_hit.astype(BF)

    g_slots = dot(slot_low, out_grad).astype(BF)
    w_send = jnp.concatenate(
        [jnp.transpose(w_qkv, (1, 0, 2)).reshape(3 * shard, cols), w_o.reshape(wo_rows * 2, cols)], 0
    )
    w_rows = w_send.shape[0]
    send_one = jnp.concatenate(
        [jnp.broadcast_to(w_send[None], (n_dp, w_rows, cols)), g_slots.reshape(n_dp, cap * 2, cols)], 1
    )
    got_one = lax.all_to_all(send_one, "dp", 0, 0)

    xf = tokens.astype(F32)
    scale_one = lax.rsqrt(jnp.mean(xf * xf, axis=-1, keepdims=True) + EPSILON)
    hat_one = xf * scale_one
    first_rows = (hat_one * gain_attn).astype(BF)
    first_all = lax.all_gather(first_rows, "tensor", axis=0, tiled=True)

    w_q3 = [got_one[:, c * shard : (c + 1) * shard].reshape(width, cols) for c in range(3)]
    wo_full = got_one[:, 3 * shard : w_rows].reshape(cols, width)
    g_mine = got_one[:, w_rows:].reshape(rows, width)
    g_all = lax.all_gather(g_mine, "tensor", axis=0)

    q, k, v = [dot(first_all, w).astype(BF).reshape(seq, heads, head) for w in w_q3]

    table_local = lax.dynamic_slice_in_dim(rel_table, t * heads, heads, 1)
    bucket_hits = (offset_buckets[:, None] == jnp.arange(buckets, dtype=jnp.int32)[None, :]).astype(F32)
    offset_bias = jnp.einsum("bh,rb->hr", table_local, bucket_hits, precision=PRECISE)
    span = 2 * seq
    tiled = jnp.tile(jnp.pad(offset_bias, ((0, 0), (0, 1))), (1, seq))
    skewed = tiled[:, seq - 1 : seq - 1 + seq * (span - 1)]
    bias = skewed.reshape(heads, seq, span - 1)[:, :, :seq]
    seg = segments[0]
    same = seg[:, None] == seg[None, :]
    scores = jnp.einsum("ihd,jhd->hij", q, k, preferred_element_type=F32) + bias
    scores = jnp.where(same[None], scores, MASKED)
    top = jnp.max(scores, axis=-1, keepdims=True)
    shifted = jnp.exp(scores - top)
    probs = shifted / jnp.sum(shifted, axis=-1, keepdims=True)
    probs_low = probs.astype(BF)
    context = jnp.einsum("hij,jhd->ihd", probs_low, v, preferred_element_type=F32).reshape(seq, cols).astype(BF)
    part = dot(context, wo_full)
    keep = lax.dynamic_slice_in_dim(part, t * rows, rows, 0)
    give = lax.dynamic_slice_in_dim(part, (1 - t) * rows, rows, 0).astype(BF)
    mid = xf + (keep + swap(give).astype(F32))
    scale_two = lax.rsqrt(jnp.mean(mid * mid, axis=-1, keepdims=True) + EPSILON)
    second = mid * scale_two * gain_moe

    out_slots = dot(slot_low, second.astype(BF)).astype(BF)
    send_two = jnp.broadcast_to(out_slots.reshape(n_dp, 1, cap, width), (n_dp, n_t, cap, width))
    arrived = lax.all_to_all(send_two.reshape(n_dp * n_t, cap, width), ALL, 0, 0)
    arrived = arrived.reshape(n_dp * n_t * cap, width)
    g_rows = jnp.transpose(g_all.reshape(n_t, n_dp, cap, width), (1, 0, 2, 3)).reshape(n_dp * n_t * cap, width)

    logits_home = jnp.dot(second, router, precision=PRECISE)
    gate_home = jnp.sum(jax.nn.softmax(logits_home, axis=-1) * hits.astype(F32), axis=-1, keepdims=True)

    w1, w2 = w_in[0], w_out[0]
    pre = dot(arrived, w1)
    activated, gelu_back = jax.vjp(lambda u: jax.nn.gelu(u, approximate=False), pre)
    hidden = activated.astype(BF)
    out_part = dot(hidden, w2)
    logits = jnp.dot(arrived.astype(F32), router, precision=PRECISE)
    r_probs = jax.nn.softmax(logits, axis=-1)
    mine = (jnp.arange(experts, dtype=jnp.int32) == me).astype(F32)[None, :]
    gate = jnp.sum(r_probs * mine, axis=-1, keepdims=True)
    g_f = g_rows.astype(F32)
    grad_expert = (gate * g_f).astype(BF)
    grad_gate = jnp.sum(g_f * out_part, axis=-1, keepdims=True)
    grad_logits = grad_gate * gate * (mine - r_probs)
    grad_hidden = dot(grad_expert, w2, ((1,), (1,)))
    grad_pre = gelu_back(grad_hidden)[0].astype(BF)
    grad_disp = dot(grad_pre, w1, ((1,), (1,))) + dot(grad_logits, router, ((1,), (1,)), PRECISE)
    router_part = dot(grad_logits, arrived.astype(F32), ((0,), (0,)), PRECISE)

    both = jnp.concatenate(
        [out_part.astype(BF).reshape(n_dp * n_t, cap, width), grad_disp.astype(BF).reshape(n_dp * n_t, cap, width)], 1
    )
    r_send = jnp.pad(router_part.astype(BF).reshape(n_dp * n_t, 1, cols), ((0, 0), (0, 0), (0, width - cols)))
    got_three = lax.all_to_all(jnp.concatenate([both, r_send], 1), ALL, 0, 0)

    grad_w_out = dot(hidden, grad_expert, ((0,), (0,)))
    grad_w_in = dot(arrived, grad_pre, ((0,), (0,)))

    got_f = got_three.astype(F32)
    summed = jnp.sum(got_f.reshape(n_dp, n_t, 2 * cap + 1, width), axis=1)
    slot_out = summed[:, :cap].reshape(rows, width)
    slot_grad = summed[:, cap : 2 * cap].reshape(rows, width)
    router_piece = jnp.sum(summed[:, 2 * cap, :cols], axis=0)
    slot_f = slot_hit.astype(F32)
    expert_out = dot(slot_f, slot_out, ((0,), (0,)), PRECISE)
    grad_second = dot(slot_f, slot_grad, ((0,), (0,)), PRECISE)
    activations = (mid + gate_home * expert_out).astype(BF)
    u2 = grad_second * gain_moe
    gain_two = jnp.sum(grad_second * mid * scale_two, axis=0)
    spread = jnp.mean(u2 * mid, axis=-1, keepdims=True)
    grad_mid = out_grad.astype(F32) + (scale_two * u2 - scale_two * scale_two * scale_two * mid * spread)
    grad_attn = lax.all_gather(grad_mid.astype(BF), "tensor", axis=0, tiled=True)

    grad_w_o = dot(context, grad_attn, ((0,), (0,)))
    grad_context = dot(grad_attn, wo_full, ((1,), (1,))).astype(BF).reshape(seq, heads, head)
    grad_probs = jnp.einsum("ihd,jhd->hij", grad_context, v, preferred_element_type=F32)
    inner = jnp.sum(probs * grad_probs, axis=-1, keepdims=True)
    grad_scores = (probs * (grad_probs - inner)).astype(BF)
    grad_q = jnp.einsum("hij,jhd->ihd", grad_scores, k, preferred_element_type=F32)
    grad_k = jnp.einsum("hij,ihd->jhd", grad_scores, q, preferred_element_type=F32)
    grad_v = jnp.einsum("hij,ihd->jhd", probs_low, grad_context, preferred_element_type=F32)
    widened = jnp.pad(grad_scores.astype(F32), ((0, 0), (0, 0), (0, seq - 1)))
    flat = jnp.pad(widened.reshape(heads, seq * (span - 1)), ((0, 0), (seq - 1, 1)))
    diagonals = jnp.sum(flat.reshape(heads, seq, span), axis=1)
    grad_table = jnp.einsum("hr,rb->hb", diagonals[:, : span - 1], bucket_hits, precision=PRECISE)
    grad3 = [x.reshape(seq, cols).astype(BF) for x in (grad_q, grad_k, grad_v)]
    grad_w3 = [dot(first_all, x, ((0,), (0,))).astype(BF).reshape(n_dp, shard, cols) for x in grad3]

    grad_first = sum(dot(x, w, ((1,), (1,))) for x, w in zip(grad3, w_q3))
    keep_first = lax.dynamic_slice_in_dim(grad_first, t * rows, rows, 0)
    give_first = lax.dynamic_slice_in_dim(grad_first, (1 - t) * rows, rows, 0).astype(BF)

    hat_all = first_all.astype(F32) / gain_attn
    gain_one = jnp.sum(grad_first * hat_all, axis=0)

    tiny = jnp.concatenate(
        [router_piece, gain_one, gain_two, jnp.pad(grad_table.reshape(-1), (0, cols - heads * buckets))]
    ).astype(BF)
    send_four = jnp.concatenate(
        grad_w3
        + [
            grad_w_o.astype(BF).reshape(n_dp, wo_rows * 2, cols),
            jnp.broadcast_to(tiny.reshape(1, -1, cols), (n_dp, tiny.size // cols, cols)),
        ],
        1,
    )
    got_four = lax.all_to_all(send_four, "dp", 0, 0)

    grad_first_own = keep_first + swap(give_first).astype(F32)
    u1 = grad_first_own * gain_attn
    spread_one = jnp.mean(u1 * xf, axis=-1, keepdims=True)
    input_grad = (grad_mid + (scale_one * u1 - scale_one * scale_one * scale_one * xf * spread_one)).astype(BF)

    tiny_got = got_four[:, w_rows:].astype(F32)
    router_half = tiny_got[:, 0]
    sums = jnp.sum(tiny_got[:, 1:], axis=0).reshape(-1)
    packed = jnp.concatenate([router_half, sums.reshape(-1, cols)], 0)
    other = swap(packed)
    low, high = jnp.where(t == 0, packed, other), jnp.where(t == 0, other, packed)
    grad_router = jnp.concatenate([low[:n_dp], high[:n_dp]], 1).T
    total = (packed[n_dp:] + other[n_dp:]).reshape(-1)
    gain_one_sum, gain_two_sum = total[:width], total[width : 2 * width]
    tables = [x[-1, : heads * buckets].reshape(heads, buckets) for x in (low, high)]
    table_sum = jnp.concatenate(tables, 0).T
    weights = jnp.sum(got_four[:, :w_rows].astype(F32), axis=0)
    grad_qkv_shard = jnp.transpose(weights[: 3 * shard].reshape(3, shard, cols), (1, 0, 2))
    grad_o_shard = weights[3 * shard :].reshape(wo_rows, width)
    return (
        activations,
        input_grad,
        gain_one_sum,
        table_sum,
        grad_qkv_shard,
        grad_o_shard,
        gain_two_sum,
        grad_router,
        grad_w_in[None],
        grad_w_out[None],
    )


def solution(mesh):
    in_specs = (
        P(("dp", "tensor"), None),
        P(),
        P(),
        P("dp", None, "tensor"),
        P(("tensor", "dp"), None),
        P(),
        P(),
        P("dp", None, "tensor"),
        P("dp", "tensor", None),
        P("dp", None),
        P(),
        P(("dp", "tensor"), None),
        P(("dp", "tensor"), None),
    )
    out_specs = (
        P(("dp", "tensor"), None),
        P(("dp", "tensor"), None),
        P(),
        P(),
        P("dp", None, "tensor"),
        P(("tensor", "dp"), None),
        P(),
        P(),
        P("dp", None, "tensor"),
        P("dp", "tensor", None),
    )
    return jax.shard_map(per_device, mesh=mesh, in_specs=in_specs, out_specs=out_specs, check_vma=False)
```

time: 871 us -> 309 us (0.35)
  blocking collectives: 451 us -> 51.9 us
  waiting for transfers between devices: 164 us -> 39.6 us
  starting transfers between devices: 75.5 us -> 29 us
  local copies, waits for them, and re-layouts: 87.1 us -> 105 us
  between operations: 16.4 us -> 1.85 us
    all_gather x2, blocking collectives: 169 us -> 6.04 us  [the longest x1 3.17 us: per_device(): g_all = lax.all_gather(g_mine, 'tensor', axis=0)]
    unnamed x1 -> x0, blocking collectives: 156 us -> none
    psum x1 -> x0, waiting for transfers between devices: 140 us -> none  [per_device(): lax.psum((grad_gain_one, grad_gain_two, table_full, grad_router), ('dp',...]
    psum x1 -> x0, blocking collectives: 96 us -> none  [per_device(): lax.psum((grad_gain_one, grad_gain_two, table_full, grad_router), ('dp',...]
    unnamed x17 -> x0, starting transfers between devices: 45.7 us -> none
    all_to_all x0 -> x1, blocking collectives: none -> 43 us  [per_device(): got_three = lax.all_to_all(jnp.concatenate([both, r_send], 1), ALL, 0, 0)]
    unnamed x115 -> x151, local copies, waits for them, and re-layouts: 45.8 us -> 15.6 us
    concatenate x0 -> x1, local copies, waits for them, and re-layouts: none -> 26.8 us  [per_device(): jnp.concatenate(grad_w3 + [grad_w_o.astype(BF).reshape(n_dp, wo_rows * 2,...]
  transfers between devices with their start and end apart: 25 -> 6, of which waited for: 7 -> 4; matrix products, arithmetic and copies ran while one was open for 29% -> 13% of each run, Pallas kernels for 0% -> 0%
where the time goes in v1:
time: 309 us; the launch traced here: 305 us
  local copies, waits for them, and re-layouts  105 us (34%)
  matrix products  52.6 us (17%)
  blocking collectives  51.9 us (17%)
  waiting for transfers between devices  39.6 us (13%)
  starting transfers between devices  29 us (9%)
  other arithmetic  24.7 us (8%)
    all_to_all x1, blocking collectives, per_device(): got_three = lax.all_to_all(jnp.concatenate([both, r_send], 1), ALL, 0, 0)  43 us
    dot_general x24, matrix products, dot(): lax.dot_general(left, right, (dims, ((), ())), precision=precision, prefe...  39.8 us
    concatenate x1, local copies, waits for them, and re-layouts, per_device(): jnp.concatenate(grad_w3 + [grad_w_o.astype(BF).reshape(n_dp, wo_rows * 2,...  26.8 us
    all_to_all x1, waiting for transfers between devices, per_device(): got_four = lax.all_to_all(send_four, 'dp', 0, 0)  25 us
    unnamed x151, local copies, waits for them, and re-layouts  15.6 us
    all_to_all x1, starting transfers between devices, per_device(): got_one = lax.all_to_all(send_one, 'dp', 0, 0)  12.3 us
    all_to_all x1, waiting for transfers between devices, per_device(): got_one = lax.all_to_all(send_one, 'dp', 0, 0)  12 us
    reshape x1, local copies, waits for them, and re-layouts, per_device(): bias = skewed.reshape(heads, seq, span - 1)[:, :, :seq]  6.43 us
  transfers between devices with their start and end apart: 6, of which 4 were waited for; matrix products, arithmetic and copies ran while one was open for 13% of the time, Pallas kernels for 0%

profile of v1, /device:TPU:1, one launch (start us, length us, event | category | flops | bytes accessed | tf_op | source)
XLA Modules:
  0.0 304.9 jit_solution(8595821904229797121)
XLA Ops:
  6.2 1.9 pad_maximum_fusion
  8.1 12.3 %all-to-all-start = ((bf16[64,52,384]{2,1,0:T(8,128)(2,1)}), bf16[64,52,384]{2,1,0:T(8,128)(2,1)}, u32[]{:S(2)}, u32[]{:S(2)}) async-start(bf16[64,52,384]{2,1,0:T(8,128)(2,1)} %pad_maximum_fusion), calls=%async_computation | async-start | bytes 5505024 | tf_op jit(solution)/shard_map/all_to_all | solution.py:55
  21.2 1.9 copy.185
  23.1 3.2 %slice.107 = f32[6,130816]{1,0:T(8,128)} slice(f32[6,131072]{1,0:T(8,128)S(1)} %bitcast.121), slice={[0:6], [255:131071]} | slice | bytes 6279168 | tf_op jit(solution)/shard_map/slice | solution.py:75
  26.2 6.4 %reshape.264 = f32[6,256,511]{2,1,0:T(8,128)} reshape(f32[6,130816]{1,0:T(8,128)} %slice.107) | data formatting | bytes 6279168 | tf_op jit(solution)/shard_map/reshape | solution.py:76
  32.7 2.7 slice.108
  35.4 3.1 %copy.183 = f32[6,256,256]{1,2,0:T(8,128)} copy(f32[6,256,256]{2,1,0:T(8,128)} %slice.108) | data formatting | bytes 3145728
  39.2 2.9 all_gather.9
  42.9 12.0 %all-to-all-done = bf16[64,52,384]{2,1,0:T(8,128)(2,1)} async-done(((bf16[64,52,384]{2,1,0:T(8,128)(2,1)}), bf16[64,52,384]{2,1,0:T(8,128)(2,1)}, u32[]{:S(2)}, u32[]{:S(2)}) %all-to-all-start) | async-done | bytes 2555936 | tf_op jit(solution)/shard_map/all_to_all | solution.py:55
  54.8 4.1 %fusion.73 = (bf16[64,12,384]{2,1,0:T(8,128)(2,1)}, bf16[64,12,384]{2,1,0:T(8,128)(2,1)}, bf16[64,12,384]{2,1,0:T(8,128)(2,1)}, bf16[64,12,384]{2,1,0:T(8,128)(2,1)}) fusion(bf16[64,52,384]{2,1,0:T(8,128)(2,1)} %all-to-all-done), kind=kLoop, calls=%fused_computation.156 | loop fusion | bytes 4718592 | tf_op jit(solution)/shard_map/slice | solution.py:64
  58.9 2.2 reshape.265
  63.5 1.8 copy.161
  67.5 1.7 copy.160
  69.3 2.1 reshape.258
  71.3 2.1 convolution_convert_fusion.13
  73.4 1.7 copy.159
  75.2 2.0 add_select_fusion
  77.2 1.7 fusion.77
  78.9 3.2 %convolution_convert_fusion.10 = bf16[6,64,256]{2,1,0:T(8,128)(2,1)} fusion(bf16[256,6,64]{0,2,1:T(8,128)(2,1)} %bitcast.140, f32[6,256]{1,0:T(8,128)S(1)} %get-tuple-element.104, f32[6,256,256]{1,2,0:T(8,128)} %copy-done.7), kind=kOutput, calls=%fused_computation.59 | convolution fusion | flops 51611392 | bytes 1972224 | tf_op jit(solution)/shard_map/hij,jhd->ihd/dot_general | solution.py:85
  84.3 3.0 collective-permute-start
  92.6 6.0 %all-to-all-start.1 = ((bf16[128,2,768]{2,1,0:T(2,128)(2,1)}), bf16[128,2,768]{2,1,0:T(2,128)(2,1)}, u32[]{:S(2)}, u32[]{:S(2)}) async-start(bf16[128,2,768]{2,1,0:T(2,128)(2,1)} %bitcast.8), calls=%async_computation.1 | async-start | bytes 786432 | tf_op jit(solution)/shard_map/all_to_all | solution.py:95
  100.3 3.2 %all_gather.10 = bf16[2,128,768]{2,1,0:T(8,128)(2,1)S(1)} all-gather(bf16[1,128,768]{2,1,0:T(8,128)(2,1)S(1)} %all_gather_reshape.3), channel_id=1, replica_groups=mesh['dp'=64,'tensor'=2] {'tensor'}, dimensions={0}, use_global_device_ids=true | all-gather | bytes 589824 | tf_op jit(solution)/shard_map/all_gather | solution.py:66
  106.4 2.6 reshape.286
  109.0 1.5 all-to-all-done.1
  117.0 5.1 %multiply_convert_fusion.1 = (bf16[256,1536]{1,0:T(8,128)(2,1)S(1)}, f32[256,1536]{1,0:T(8,128)}, f32[256,1536]{1,0:T(8,128)}) fusion(bf16[256,768]{1,0:T(8,128)(2,1)S(1)} %reshape.267, bf16[1,768,1536]{2,1,0:T(8,128)(2,1)S(1)} %copy-done), kind=kOutput, calls=%fused_computation.25 | convolution fusion | flops 629538816 | bytes 6684672 | tf_op jit(solution)/shard_map/dot_general | solution.py:19
  122.2 1.5 fusion.75
  124.8 1.8 fusion.53
  126.6 1.5 copy.164
  130.6 1.9 convert_element_type.221
  132.5 1.9 reshape.268
  134.4 1.6 reshape.293
  136.0 3.8 %add_convert_fusion = bf16[256,1536]{1,0:T(8,128)(2,1)S(1)} fusion(f32[256,1536]{1,0:T(8,128)} %get-tuple-element.85, bf16[256,768]{1,0:T(8,128)(2,1)} %convert_element_type.221, bf16[1,1536,768]{2,1,0:T(8,128)(2,1)} %param.21, f32[256,1536]{1,0:T(8,128)} %get-tuple-element.106), kind=kOutput, calls=%fused_computation.24 | convolution fusion | flops 609484800 | bytes 6684672 | tf_op jit(solution)/shard_map/dot_general | solution.py:19
  140.7 1.6 fusion.24
  143.4 2.2 fusion.12
  145.7 43.0 %all_to_all.20 = bf16[128,5,768]{2,1,0:T(8,128)(2,1)S(1)} all-to-all(bf16[128,5,768]{2,1,0:T(8,128)(2,1)S(1)} %fusion.12), channel_id=1, replica_groups=mesh['dp'=64,'tensor'=2] {'dp','tensor'}, dimensions={0} | all-to-all | bytes 1966080 | tf_op jit(solution)/shard_map/all_to_all | solution.py:124
  193.1 2.9 all_gather.11
  197.7 3.2 %convolution_convert_fusion.6 = bf16[6,64,256]{2,1,0:T(8,128)(2,1)} fusion(bf16[256,6,64]{0,2,1:T(8,128)(2,1)S(1)} %bitcast.142, f32[6,256]{1,0:T(8,128)S(1)} %get-tuple-element.104, f32[6,256,256]{1,2,0:T(8,128)} %copy-done.7), kind=kOutput, calls=%fused_computation.55 | convolution fusion | flops 51611392 | bytes 1972224 | tf_op jit(solution)/shard_map/hij,ihd->jhd/dot_general | solution.py:151
  203.9 2.3 fusion.81
  209.8 2.1 reshape.278
  217.4 3.9 %reshape.307 = bf16[784896]{0:T(1024)(128)(2,1)} reshape(bf16[6,256,511]{2,1,0:T(8,128)(2,1)S(1)} %pad.25.clone) | data formatting | bytes 3139584
  221.3 3.0 reshape.280
  225.1 1.6 bitcast_reduce_fusion
  227.2 26.8 %concatenate.29 = bf16[64,54,384]{2,1,0:T(8,128)(2,1)} concatenate(bf16[64,12,384]{2,1,0:T(8,128)(2,1)S(1)} %copy-done.19, bf16[64,12,384]{2,1,0:T(8,128)(2,1)} %reshape.277, bf16[64,12,384]{2,1,0:T(8,128)(2,1)S(1)} %copy-done.18, bf16[64,12,384]{2,1,0:T(8,128)(2,1)S(1)} %copy-done.17, bf16[64,6,384]{2,1,0:T(8,128)(2,1)S(1)} %broadcast_in_dim.29), dimensions={1} | concatenate | bytes 5308416 | tf_op jit(solution)/shard_map/concatenate | solution.py:169
  254.1 5.9 %all-to-all-start.3 = ((bf16[64,54,384]{2,1,0:T(8,128)(2,1)}), bf16[64,54,384]{2,1,0:T(8,128)(2,1)}, u32[]{:S(2)}, u32[]{:S(2)}) async-start(bf16[64,54,384]{2,1,0:T(8,128)(2,1)} %concatenate.29), calls=%async_computation.3 | async-start | bytes 5505024 | tf_op jit(solution)/shard_map/all_to_all | solution.py:177
  260.8 3.0 convolution_bitcast_fusion.1
  263.8 3.1 %convolution_bitcast_fusion = f32[1,1536,768]{2,1,0:T(8,128)} fusion(bf16[256,1536]{1,0:T(8,128)(2,1)S(1)} %copy-done.6, f32[256,768]{1,0:T(8,128)S(1)} %copy-done.4, f32[256]{0:T(256)S(1)} %copy-done.52), kind=kOutput, calls=%fused_computation.2 | convolution fusion | flops 604372992 | bytes 6292480 | tf_op jit(solution)/shard_map/dot_general | solution.py:19
  270.9 25.0 %all-to-all-done.3 = bf16[64,54,384]{2,1,0:T(8,128)(2,1)} async-done(((bf16[64,54,384]{2,1,0:T(8,128)(2,1)}), bf16[64,54,384]{2,1,0:T(8,128)(2,1)}, u32[]{:S(2)}, u32[]{:S(2)}) %all-to-all-start.3) | async-done | bytes 2654240 | tf_op jit(solution)/shard_map/all_to_all | solution.py:177
  298.6 2.0 convert_reduce_fusion
  (257 shorter events, 67.1 us)
Async XLA Ops:
  0.6 116.4 %copy-start = (bf16[1,768,1536]{2,1,0:T(8,128)(2,1)S(1)}, bf16[1,768,1536]{2,1,0:T(8,128)(2,1)}, u32[]{:S(2)}) copy-start(bf16[1,768,1536]{2,1,0:T(8,128)(2,1)} %param.20) | copy-start | bytes 7077892
  8.1 12.3 %copy-start.69 = (f32[32,12]{0,1:T(8,128)S(1)}, f32[32,12]{0,1:T(8,128)}, u32[]{:S(2)}) copy-start(f32[32,12]{0,1:T(8,128)} %param.15) | copy-start | bytes 4612
  8.1 12.4 %copy-start.70 = (s32[511]{0:T(512)S(1)}, s32[511]{0:T(512)}, u32[]{:S(2)}) copy-start(s32[511]{0:T(512)} %param.23) | copy-start | bytes 6136
  8.1 46.7 %all-to-all-start = ((bf16[64,52,384]{2,1,0:T(8,128)(2,1)}), bf16[64,52,384]{2,1,0:T(8,128)(2,1)}, u32[]{:S(2)}, u32[]{:S(2)}) async-start(bf16[64,52,384]{2,1,0:T(8,128)(2,1)} %pad_maximum_fusion), calls=%async_computation | async-start | bytes 5505024 | tf_op jit(solution)/shard_map/all_to_all | solution.py:55
  35.4 3.1 %copy-start.15 = (bf16[128,768]{1,0:T(8,128)(2,1)S(1)}, bf16[128,768]{1,0:T(8,128)(2,1)}, u32[]{:S(2)}) copy-start(bf16[128,768]{1,0:T(8,128)(2,1)} %param.13) | copy-start | bytes 589828
  35.4 3.7 %copy-start.46 = (f32[768]{0:T(1024)S(1)}, f32[768]{0:T(1024)}, u32[]{:S(2)}) copy-start(f32[768]{0:T(1024)} %param.14) | copy-start | bytes 9220
  35.4 6.7 %copy-start.64 = (s32[1,256]{1,0:T(1,128)S(1)}, s32[1,256]{1,0:T(1,128)}, u32[]{:S(2)}) copy-start(s32[1,256]{1,0:T(1,128)} %param.22) | copy-start | bytes 3076
  39.1 19.8 %copy-start.65 = (f32[128]{0:T(128)}, f32[128]{0:T(128)S(1)}, u32[]{:S(2)}) copy-start(f32[128]{0:T(128)S(1)} %get-tuple-element.101) | copy-start | bytes 1540
  62.4 2.8 copy-start.13
  66.5 7.0 %copy-start.9 = (bf16[768,384]{1,0:T(8,128)(2,1)}, bf16[768,384]{1,0:T(8,128)(2,1)S(1)}, u32[]{:S(2)}) copy-start(bf16[768,384]{1,0:T(8,128)(2,1)S(1)} %reshape.260) | copy-start | bytes 1769476
  78.9 3.2 %copy-start.11 = (bf16[384,768]{1,0:T(8,128)(2,1)S(1)}, bf16[384,768]{1,0:T(8,128)(2,1)}, u32[]{:S(2)}) copy-start(bf16[384,768]{1,0:T(8,128)(2,1)} %reshape.265) | copy-start | bytes 1769476
  82.1 8.6 %copy-start.45 = (f32[768]{0:T(1024)S(1)}, f32[768]{0:T(1024)}, u32[]{:S(2)}) copy-start(f32[768]{0:T(1024)} %param.18) | copy-start | bytes 9220
  84.3 4.1 %collective-permute-start = (bf16[128,768]{1,0:T(8,128)(2,1)S(1)}, bf16[128,768]{1,0:T(8,128)(2,1)S(1)}, u32[]{:S(2)}, u32[]{:S(2)}) collective-permute-start(bf16[128,768]{1,0:T(8,128)(2,1)S(1)} %dynamic-slice_convert_fusion.1), channel_id=1, source_target_pairs={{0,1},{1,0},{2,3},{3,2},{4,5},{5,4},{6,7},{7,6},{8,9},{9,8},{10,11... | collective-permute-start | bytes 589832 | tf_op jit(solution)/shard_map/ppermute | solution.py:15
  92.6 17.9 %all-to-all-start.1 = ((bf16[128,2,768]{2,1,0:T(2,128)(2,1)}), bf16[128,2,768]{2,1,0:T(2,128)(2,1)}, u32[]{:S(2)}, u32[]{:S(2)}) async-start(bf16[128,2,768]{2,1,0:T(2,128)(2,1)} %bitcast.8), calls=%async_computation.1 | async-start | bytes 786432 | tf_op jit(solution)/shard_map/all_to_all | solution.py:95
  117.0 5.1 %copy-start.3 = (f32[256,768]{1,0:T(8,128)S(1)}, f32[256,768]{1,0:T(8,128)}, u32[]{:S(2)}) copy-start(f32[256,768]{1,0:T(8,128)} %reshape.286) | copy-start | bytes 2359300
  117.0 5.1 %copy-start.22 = (bf16[1,1536,768]{2,1,0:T(8,128)(2,1)S(1)}, bf16[1,1536,768]{2,1,0:T(8,128)(2,1)}, u32[]{:S(2)}) copy-start(bf16[1,1536,768]{2,1,0:T(8,128)(2,1)} %param.21) | copy-start | bytes 7077892
  122.2 2.6 copy-start.30
  136.0 4.7 %copy-start.39 = (f32[256,768]{1,0:T(8,128)S(1)}, f32[256,768]{1,0:T(8,128)}, u32[]{:S(2)}) copy-start(f32[256,768]{1,0:T(8,128)} %fusion.53) | copy-start | bytes 2359300
  189.8 2.4 copy-start.38
  191.1 4.8 %copy-start.12 = (bf16[384,768]{1,0:T(8,128)(2,1)S(1)}, bf16[384,768]{1,0:T(8,128)(2,1)}, u32[]{:S(2)}) copy-start(bf16[384,768]{1,0:T(8,128)(2,1)} %reshape.265) | copy-start | bytes 1769476
  192.1 4.2 %copy-start.37 = (bf16[6,64,256]{2,1,0:T(8,128)(2,1)S(1)}, bf16[6,64,256]{2,1,0:T(8,128)(2,1)}, u32[]{:S(2)}) copy-start(bf16[6,64,256]{2,1,0:T(8,128)(2,1)} %convolution_convert_fusion.10) | copy-start | bytes 589828
  197.7 3.2 %copy-start.8 = (f32[6,256,256]{1,2,0:T(8,128)S(1)}, f32[6,256,256]{1,2,0:T(8,128)}, u32[]{:S(2)}) copy-start(f32[6,256,256]{1,2,0:T(8,128)} %get-tuple-element.105) | copy-start | bytes 4718596
  197.7 3.2 %copy-start.44 = (bf16[256,384]{0,1:T(8,128)(2,1)S(1)}, bf16[256,384]{0,1:T(8,128)(2,1)}, u32[]{:S(2)}) copy-start(bf16[256,384]{0,1:T(8,128)(2,1)} %copy.159) | copy-start | bytes 589828
  203.9 2.3 copy-start.29
  203.9 3.5 %copy-start.24 = (bf16[384,768]{1,0:T(8,128)(2,1)S(1)}, bf16[384,768]{1,0:T(8,128)(2,1)}, u32[]{:S(2)}) copy-start(bf16[384,768]{1,0:T(8,128)(2,1)} %convolution_convert_fusion) | copy-start | bytes 1769476
  206.2 2.4 copy-start.42
  209.8 3.4 %copy-start.14 = (bf16[768,384]{1,0:T(8,128)(2,1)S(1)}, bf16[768,384]{1,0:T(8,128)(2,1)}, u32[]{:S(2)}) copy-start(bf16[768,384]{1,0:T(8,128)(2,1)} %copy-done.13) | copy-start | bytes 1769476
  209.8 3.4 %copy-start.20 = (f32[256,768]{1,0:T(8,128)S(1)}, f32[256,768]{1,0:T(8,128)}, u32[]{:S(2)}) copy-start(f32[256,768]{1,0:T(8,128)} %fusion.81) | copy-start | bytes 2359300
  225.1 2.2 copy-start.17
  225.1 2.2 copy-start.18
  254.1 6.0 %copy-start.31 = (f32[768,64]{0,1:T(8,128)S(1)}, f32[768,64]{0,1:T(8,128)}, u32[]{:S(2)}) copy-start(f32[768,64]{0,1:T(8,128)} %param.19) | copy-start | bytes 589828
  254.1 6.0 %copy-start.56 = (f32[128]{0:T(128)S(1)}, f32[128]{0:T(128)}, u32[]{:S(2)}) copy-start(f32[128]{0:T(128)} %copy-done.53) | copy-start | bytes 1540
  254.1 6.6 %copy-start.61 = (s32[128,1]{0,1:T(1,128)S(1)}, s32[128,1]{0,1:T(1,128)}, u32[]{:S(2)}) copy-start(s32[128,1]{0,1:T(1,128)} %param.24) | copy-start | bytes 1540
  254.1 6.7 %copy-start.41 = (bf16[256,1536]{1,0:T(8,128)(2,1)S(1)}, bf16[256,1536]{1,0:T(8,128)(2,1)}, u32[]{:S(2)}) copy-start(bf16[256,1536]{1,0:T(8,128)(2,1)} %copy-done.40) | copy-start | bytes 2359300
  254.1 41.8 %all-to-all-start.3 = ((bf16[64,54,384]{2,1,0:T(8,128)(2,1)}), bf16[64,54,384]{2,1,0:T(8,128)(2,1)}, u32[]{:S(2)}, u32[]{:S(2)}) async-start(bf16[64,54,384]{2,1,0:T(8,128)(2,1)} %concatenate.29), calls=%async_computation.3 | async-start | bytes 5505024 | tf_op jit(solution)/shard_map/all_to_all | solution.py:177
  260.8 3.0 copy-start.4
  260.8 3.0 copy-start.6
  260.8 3.0 copy-start.52
  263.8 3.1 %copy-start.34 = (f32[64,2,768]{2,1,0:T(2,128)S(1)}, f32[64,2,768]{2,1,0:T(2,128)}, u32[]{:S(2)}) copy-start(f32[64,2,768]{2,1,0:T(2,128)} %get-tuple-element.93) | copy-start | bytes 1179652
  263.8 5.0 %copy-start.59 = (s32[128]{0:T(128)S(1)}, s32[128]{0:T(128)}, u32[]{:S(2)}) copy-start(s32[128]{0:T(128)} %copy-done.57) | copy-start | bytes 1540
  266.9 3.0 copy-start.16
  266.9 3.0 copy-start.36
  266.9 3.2 %copy-start.35 = (f32[128,768]{1,0:T(8,128)S(1)}, f32[128,768]{1,0:T(8,128)}, u32[]{:S(2)}) copy-start(f32[128,768]{1,0:T(8,128)} %get-tuple-element.83) | copy-start | bytes 1179652
  266.9 3.2 %copy-start.66 = (f32[128]{0:T(128)S(1)}, f32[128]{0:T(128)}, u32[]{:S(2)}) copy-start(f32[128]{0:T(128)} %copy-done.65) | copy-start | bytes 1540
  266.9 3.2 %copy-start.68 = (f32[128]{0:T(128)S(1)}, f32[128]{0:T(128)}, u32[]{:S(2)}) copy-start(f32[128]{0:T(128)} %get-tuple-element.100) | copy-start | bytes 1540
  268.3 1.5 collective-permute-start.1
  297.2 7.5 %copy-start.1 = (bf16[1,768,1536]{2,1,0:T(8,128)(2,1)S(1)}, bf16[1,768,1536]{2,1,0:T(8,128)(2,1)}, u32[]{:S(2)}) copy-start(bf16[1,768,1536]{2,1,0:T(8,128)(2,1)} %param.20) | copy-start | bytes 7077892
  297.2 4.7 %collective-permute-start.2 = (f32[69,384]{1,0:T(8,128)S(1)}, f32[69,384]{1,0:T(8,128)S(1)}, u32[]{:S(2)}, u32[]{:S(2)}) collective-permute-start(f32[69,384]{1,0:T(8,128)S(1)} %pad_maximum_fusion.1), channel_id=1, source_target_pairs={{0,1},{1,0},{2,3},{3,2},{4,5},{5,4},{6,7},{7,6},{8,9},{9,8},{10,11... | collective-permute-start | bytes 317960 | tf_op jit(solution)/shard_map/ppermute | solution.py:15
  (30 other events, 41.2 us)

commit v2 on v1

--- a/solution.py
+++ b/solution.py
@@ -1,6 +1,8 @@
 import jax
 import jax.numpy as jnp
 from jax import lax
+from jax.experimental import pallas as pl
+from jax.experimental.pallas import tpu as pltpu
 from jax.sharding import PartitionSpec as P
 
 PRECISE = lax.Precision.HIGHEST
@@ -17,6 +19,182 @@
 
 def dot(left, right, dims=((1,), (0,)), precision=None):
     return lax.dot_general(left, right, (dims, ((), ())), precision=precision, preferred_element_type=F32)
+
+
+def dot_t(left, right):
+    return dot(left, right, ((1,), (1,)))
+
+
+def vmem(limit_mb, flops, moved):
+    return dict(
+        compiler_params=pltpu.CompilerParams(vmem_limit_bytes=limit_mb * 1024 * 1024),
+        cost_estimate=pl.CostEstimate(flops=flops, bytes_accessed=moved, transcendentals=0),
+    )
+
+
+WHOLE = pl.BlockSpec(memory_space=pltpu.VMEM)
+SCALAR = pl.BlockSpec(memory_space=pltpu.SMEM)
+ANYWHERE = pl.BlockSpec(memory_space=pl.ANY)
+
+
+def groups(ref):
+    return [ref[:, 16 * g : 16 * g + 16, :].reshape(ref.shape[0] * 16, ref.shape[2]) for g in range(3)]
+
+
+def attend_kernel(t_ref, got_ref, x_ref, so_ref, bias_ref, keep_ref, give_ref, ctx_ref, qkv_ref, probs_ref, wo_ref):
+    one, two, three = groups(got_ref)
+    q = (dot(x_ref[0], one) + dot(x_ref[2], three)).astype(BF)
+    k = (dot(x_ref[1], one) + dot(x_ref[3], three)).astype(BF)
+    v = (dot(x_ref[0], two) + dot(x_ref[4], three)).astype(BF)
+    qkv_ref[0], qkv_ref[1], qkv_ref[2] = q, k, v
+    cols = q.shape[1]
+    for half in range(2):
+        wo_ref[:, half * cols : half * cols + cols] = (
+            dot(so_ref[half], two) + dot(so_ref[2 + half], three)
+        ).astype(BF)
+    lane = lax.broadcasted_iota(jnp.int32, (q.shape[0], 128), 1)
+    zero = jnp.zeros((q.shape[0], 128), BF)
+    for pair in range(cols // 128):
+        at = slice(128 * pair, 128 * pair + 128)
+        q2, k2, v2 = q[:, at], k[:, at], v[:, at]
+        outs = []
+        for which in range(2):
+            mine = (lane < 64) if which == 0 else (lane >= 64)
+            scores = dot_t(jnp.where(mine, q2, zero), k2) + bias_ref[2 * pair + which]
+            top = jnp.max(scores, axis=-1, keepdims=True)
+            shifted = jnp.exp(scores - top)
+            probs = (shifted * (1.0 / jnp.sum(shifted, axis=-1, keepdims=True))).astype(BF)
+            probs_ref[2 * pair + which] = probs
+            outs.append(dot(probs, v2))
+        ctx_ref[:, at] = jnp.where(lane < 64, outs[0], outs[1]).astype(BF)
+    part = dot(ctx_ref[...], wo_ref[...])
+    rows = part.shape[0] // 2
+    low, high = part[:rows], part[rows:]
+    first = t_ref[0] == 0
+    keep_ref[...] = jnp.where(first, low, high)
+    give_ref[...] = jnp.where(first, high, low).astype(BF)
+
+
+def attend(t, got, x, so, bias):
+    cols, seq = got.shape[2], x.shape[1]
+    heads = bias.shape[0]
+    shape = jax.ShapeDtypeStruct
+    return pl.pallas_call(
+        attend_kernel,
+        in_specs=[SCALAR] + [WHOLE] * 4,
+        out_specs=[WHOLE] * 6,
+        out_shape=[
+            shape((seq // 2, 2 * cols), F32),
+            shape((seq // 2, 2 * cols), BF),
+            shape((seq, cols), BF),
+            shape((3, seq, cols), BF),
+            shape((heads, seq, seq), BF),
+            shape((cols, 2 * cols), BF),
+        ],
+        **vmem(50, 4_000_000_000, 14_000_000),
+    )(t, got, x, so, bias)
+
+
+def attend_back_kernel(
+    ga_ref, wo_ref, qkv_ref, probs_ref, hits_ref, gain_ref, router_ref, two_ref, got_any, xt_any, xot_any, s_any,
+    send_ref, g3_ref, got_ref, xt_ref, xot_ref, s_ref, sems,
+):
+    moves = [
+        pltpu.make_async_copy(source, target, sems.at[i])
+        for i, (source, target) in enumerate([(xt_any, xt_ref), (xot_any, xot_ref), (got_any, got_ref), (s_any, s_ref)])
+    ]
+    for move in moves:
+        move.start()
+    ga = ga_ref[...]
+    q, k, v = qkv_ref[0], qkv_ref[1], qkv_ref[2]
+    seq, cols = q.shape
+    gctx = dot_t(ga, wo_ref[...]).astype(BF)
+    lane = lax.broadcasted_iota(jnp.int32, (seq, 128), 1)
+    low = lane < 64
+    zero = jnp.zeros((seq, 128), BF)
+    row8 = lax.broadcasted_iota(jnp.int32, (8, 2 * seq), 0)
+    along = [lax.broadcasted_iota(jnp.int32, (seq, seq), axis) for axis in range(2)]
+    flip = (along[0] + along[1] == seq - 1).astype(F32).astype(BF)
+    diagonals = jnp.zeros((8, 2 * seq), F32)
+    for pair in range(cols // 128):
+        at = slice(128 * pair, 128 * pair + 128)
+        q2, k2, v2, c2 = q[:, at], k[:, at], v[:, at], gctx[:, at]
+        parts = []
+        for which in range(2):
+            mine = low if which == 0 else jnp.logical_not(low)
+            probs = probs_ref[2 * pair + which]
+            probs_f = probs.astype(F32)
+            grad_probs = dot_t(jnp.where(mine, c2, zero), v2)
+            inner = jnp.sum(probs_f * grad_probs, axis=-1, keepdims=True)
+            ds = (probs_f * (grad_probs - inner)).astype(BF)
+            parts.append((dot(ds, k2), dot(ds.T, q2), dot(probs.T, c2)))
+            wide = jnp.concatenate([dot(flip, ds), jnp.zeros((seq, seq), F32)], 1)
+            rolled = pltpu.roll(wide, 0, 1, stride=1, stride_axis=0)
+            sums = jnp.sum(rolled, axis=0, keepdims=True)
+            diagonals = jnp.where(row8 == 2 * pair + which, sums, diagonals)
+        for c in range(3):
+            g3_ref[c, :, at] = jnp.where(low, parts[0][c], parts[1][c]).astype(BF)
+    gq, gk, gv = g3_ref[0], g3_ref[1], g3_ref[2]
+    ga0, ga1 = ga[:, :cols], ga[:, cols:]
+    moves[0].wait()
+    moves[1].wait()
+    one = dot(xt_ref[0], gq) + dot(xt_ref[1], gk)
+    two = dot(xt_ref[0], gv) + dot(xot_ref[0], ga0) + dot(xot_ref[1], ga1)
+    three = (
+        dot(xt_ref[2], gq) + dot(xt_ref[3], gk) + dot(xt_ref[4], gv) + dot(xot_ref[2], ga0) + dot(xot_ref[3], ga1)
+    )
+    moves[2].wait()
+    moves[3].wait()
+    gain = jnp.zeros((128, gain_ref.shape[1]), F32)
+    for g, (grad, weight) in enumerate(zip((one, two, three), groups(got_ref))):
+        send_ref[:, 16 * g : 16 * g + 16, :] = grad.astype(BF).reshape(send_ref.shape[0], 16, cols)
+        product = grad * weight.astype(F32)
+        product = (product[:, :128] + product[:, 128:256] + product[:, 256:]).astype(BF)
+        gain = gain + dot(product.T, s_ref[g])
+    gain = jnp.sum(gain, axis=0, keepdims=True) / gain_ref[...]
+    table = jnp.dot(diagonals, hits_ref[...], precision=PRECISE, preferred_element_type=F32)
+    head_of = lax.broadcasted_iota(jnp.int32, table.shape, 1) // 64
+    table = jnp.sum(
+        jnp.where(head_of == lax.broadcasted_iota(jnp.int32, table.shape, 0), table, 0.0), axis=0, keepdims=True
+    )
+    gain_two = two_ref[...]
+    row = lax.broadcasted_iota(jnp.int32, (8, cols), 0)
+    tiny = jnp.zeros((8, cols), F32)
+    for i, value in enumerate(
+        (router_ref[...], gain[:, :cols], gain[:, cols:], gain_two[:, :cols], gain_two[:, cols:], table)
+    ):
+        tiny = jnp.where(row == i, value, tiny)
+    send_ref[:, 48:56, :] = jnp.broadcast_to(tiny.astype(BF)[None], (send_ref.shape[0], 8, cols))
+
+
+def attend_back(ga, wo, qkv, probs, hits, gain, router, two, got, xt, xot, s):
+    _, seq, cols = qkv.shape
+    shape = jax.ShapeDtypeStruct
+    return pl.pallas_call(
+        attend_back_kernel,
+        in_specs=[WHOLE] * 8 + [ANYWHERE] * 4,
+        out_specs=[WHOLE] * 2,
+        out_shape=[shape(got.shape, BF), shape((3, seq, cols), BF)],
+        scratch_shapes=[pltpu.VMEM(a.shape, BF) for a in (got, xt, xot, s)] + [pltpu.SemaphoreType.DMA((4,))],
+        **vmem(50, 4_000_000_000, 16_000_000),
+    )(ga, wo, qkv, probs, hits, gain, router, two, got, xt, xot, s)
+
+
+def selections(n_dp, shard, cols, wo_rows):
+    width = n_dp * shard
+    d = jnp.arange(width, dtype=jnp.int32)[None, :, None]
+    row = jnp.arange(n_dp * 16, dtype=jnp.int32)[None, None, :]
+    start = jnp.array([0, 8, -8, -4, 0], jnp.int32)[:, None, None]
+    big = jnp.array([False, False, True, True, True])[:, None, None]
+    i = d % shard
+    sel = (row == (d // shard) * 16 + i + start) & ((i >= 8) == big)
+    d = jnp.arange(cols, dtype=jnp.int32)[None, :, None]
+    half = jnp.array([0, 1, 0, 1], jnp.int32)[:, None, None]
+    late = jnp.array([False, False, True, True])[:, None, None]
+    i = d % wo_rows
+    place = jnp.where(late, 12 + 2 * (i - 4), 8 + 2 * i) + half
+    so = (row == (d // wo_rows) * 16 + place) & ((i >= 4) == late)
+    return sel.astype(BF), so.astype(BF)
 
 
 def per_device(
@@ -45,12 +223,15 @@
     slot_low = slot_hit.astype(BF)
 
     g_slots = dot(slot_low, out_grad).astype(BF)
-    w_send = jnp.concatenate(
-        [jnp.transpose(w_qkv, (1, 0, 2)).reshape(3 * shard, cols), w_o.reshape(wo_rows * 2, cols)], 0
-    )
+    pieces = [w_qkv[:, 0], w_qkv[:, 1], w_qkv[:, 2], w_o.reshape(wo_rows * 2, cols)]
+    w_send = jnp.concatenate([x[:8] for x in pieces] + [x[8:] for x in pieces], 0)
     w_rows = w_send.shape[0]
     send_one = jnp.concatenate(
-        [jnp.broadcast_to(w_send[None], (n_dp, w_rows, cols)), g_slots.reshape(n_dp, cap * 2, cols)], 1
+        [
+            jnp.broadcast_to(w_send[None], (n_dp, w_rows, cols)),
+            jnp.pad(g_slots.reshape(n_dp, cap * 2, cols), ((0, 0), (0, 8 - cap * 2), (0, 0))),
+        ],
+        1,
     )
     got_one = lax.all_to_all(send_one, "dp", 0, 0)
 
@@ -60,12 +241,10 @@
     first_rows = (hat_one * gain_attn).astype(BF)
     first_all = lax.all_gather(first_rows, "tensor", axis=0, tiled=True)
 
-    w_q3 = [got_one[:, c * shard : (c + 1) * shard].reshape(width, cols) for c in range(3)]
-    wo_full = got_one[:, 3 * shard : w_rows].reshape(cols, width)
-    g_mine = got_one[:, w_rows:].reshape(rows, width)
+    sel, so = selections(n_dp, shard, cols, wo_rows)
+    x = jnp.stack([dot(first_all, sel[c]).astype(BF) for c in range(5)])
+    g_mine = got_one[:, w_rows : w_rows + 2 * cap].reshape(rows, width)
     g_all = lax.all_gather(g_mine, "tensor", axis=0)
-
-    q, k, v = [dot(first_all, w).astype(BF).reshape(seq, heads, head) for w in w_q3]
 
     table_local = lax.dynamic_slice_in_dim(rel_table, t * heads, heads, 1)
     bucket_hits = (offset_buckets[:, None] == jnp.arange(buckets, dtype=jnp.int32)[None, :]).astype(F32)
@@ -76,16 +255,8 @@
     bias = skewed.reshape(heads, seq, span - 1)[:, :, :seq]
     seg = segments[0]
     same = seg[:, None] == seg[None, :]
-    scores = jnp.einsum("ihd,jhd->hij", q, k, preferred_element_type=F32) + bias
-    scores = jnp.where(same[None], scores, MASKED)
-    top = jnp.max(scores, axis=-1, keepdims=True)
-    shifted = jnp.exp(scores - top)
-    probs = shifted / jnp.sum(shifted, axis=-1, keepdims=True)
-    probs_low = probs.astype(BF)
-    context = jnp.einsum("hij,jhd->ihd", probs_low, v, preferred_element_type=F32).reshape(seq, cols).astype(BF)
-    part = dot(context, wo_full)
-    keep = lax.dynamic_slice_in_dim(part, t * rows, rows, 0)
-    give = lax.dynamic_slice_in_dim(part, (1 - t) * rows, rows, 0).astype(BF)
+    bias = jnp.where(same[None], bias, MASKED)
+    keep, give, context, qkv, probs, wo_full = attend(t.reshape(1), got_one, x, so, bias)
     mid = xf + (keep + swap(give).astype(F32))
     scale_two = lax.rsqrt(jnp.mean(mid * mid, axis=-1, keepdims=True) + EPSILON)
     second = mid * scale_two * gain_moe
@@ -141,47 +312,29 @@
     grad_mid = out_grad.astype(F32) + (scale_two * u2 - scale_two * scale_two * scale_two * mid * spread)
     grad_attn = lax.all_gather(grad_mid.astype(BF), "tensor", axis=0, tiled=True)
 
-    grad_w_o = dot(context, grad_attn, ((0,), (0,)))
-    grad_context = dot(grad_attn, wo_full, ((1,), (1,))).astype(BF).reshape(seq, heads, head)
-    grad_probs = jnp.einsum("ihd,jhd->hij", grad_context, v, preferred_element_type=F32)
-    inner = jnp.sum(probs * grad_probs, axis=-1, keepdims=True)
-    grad_scores = (probs * (grad_probs - inner)).astype(BF)
-    grad_q = jnp.einsum("hij,jhd->ihd", grad_scores, k, preferred_element_type=F32)
-    grad_k = jnp.einsum("hij,ihd->jhd", grad_scores, q, preferred_element_type=F32)
-    grad_v = jnp.einsum("hij,ihd->jhd", probs_low, grad_context, preferred_element_type=F32)
-    widened = jnp.pad(grad_scores.astype(F32), ((0, 0), (0, 0), (0, seq - 1)))
-    flat = jnp.pad(widened.reshape(heads, seq * (span - 1)), ((0, 0), (seq - 1, 1)))
-    diagonals = jnp.sum(flat.reshape(heads, seq, span), axis=1)
-    grad_table = jnp.einsum("hr,rb->hb", diagonals[:, : span - 1], bucket_hits, precision=PRECISE)
-    grad3 = [x.reshape(seq, cols).astype(BF) for x in (grad_q, grad_k, grad_v)]
-    grad_w3 = [dot(first_all, x, ((0,), (0,))).astype(BF).reshape(n_dp, shard, cols) for x in grad3]
-
-    grad_first = sum(dot(x, w, ((1,), (1,))) for x, w in zip(grad3, w_q3))
+    xt = jnp.stack([dot(sel[c], first_all, ((0,), (1,))).astype(BF) for c in range(5)])
+    xot = jnp.stack([dot(so[c], context, ((0,), (1,))).astype(BF) for c in range(4)])
+    back = jnp.stack([(sel[0] + sel[1]).T, sel[0].T, (sel[2] + sel[3] + sel[4]).T])
+    hits_wide = jnp.tile(jnp.pad(bucket_hits, ((0, 1), (0, 64 - buckets))), (1, heads))
+    send_four, grad3 = attend_back(
+        grad_attn, wo_full, qkv, probs, hits_wide, gain_attn[None], router_piece[None], gain_two[None], got_one, xt, xot, back
+    )
+
+    got_four = lax.all_to_all(send_four, "dp", 0, 0)
+
+    one, two, three = [got_one[:, 16 * g : 16 * g + 16].reshape(n_dp * 16, cols) for g in range(3)]
+    spread_q, spread_k, spread_v = dot_t(grad3[0], one), dot_t(grad3[1], one), dot_t(grad3[2], two)
+    last = [dot_t(grad3[c], three).astype(BF) for c in range(3)]
+    grad_first = dot_t(spread_q.astype(BF), sel[0]) + dot_t(spread_k.astype(BF), sel[1]) + dot_t(spread_v.astype(BF), sel[0])
+    grad_first = grad_first + sum(dot_t(last[c], sel[2 + c]) for c in range(3))
     keep_first = lax.dynamic_slice_in_dim(grad_first, t * rows, rows, 0)
     give_first = lax.dynamic_slice_in_dim(grad_first, (1 - t) * rows, rows, 0).astype(BF)
-
-    hat_all = first_all.astype(F32) / gain_attn
-    gain_one = jnp.sum(grad_first * hat_all, axis=0)
-
-    tiny = jnp.concatenate(
-        [router_piece, gain_one, gain_two, jnp.pad(grad_table.reshape(-1), (0, cols - heads * buckets))]
-    ).astype(BF)
-    send_four = jnp.concatenate(
-        grad_w3
-        + [
-            grad_w_o.astype(BF).reshape(n_dp, wo_rows * 2, cols),
-            jnp.broadcast_to(tiny.reshape(1, -1, cols), (n_dp, tiny.size // cols, cols)),
-        ],
-        1,
-    )
-    got_four = lax.all_to_all(send_four, "dp", 0, 0)
-
     grad_first_own = keep_first + swap(give_first).astype(F32)
     u1 = grad_first_own * gain_attn
     spread_one = jnp.mean(u1 * xf, axis=-1, keepdims=True)
     input_grad = (grad_mid + (scale_one * u1 - scale_one * scale_one * scale_one * xf * spread_one)).astype(BF)
 
-    tiny_got = got_four[:, w_rows:].astype(F32)
+    tiny_got = got_four[:, w_rows : w_rows + 6].astype(F32)
     router_half = tiny_got[:, 0]
     sums = jnp.sum(tiny_got[:, 1:], axis=0).reshape(-1)
     packed = jnp.concatenate([router_half, sums.reshape(-1, cols)], 0)
@@ -190,11 +343,12 @@
     grad_router = jnp.concatenate([low[:n_dp], high[:n_dp]], 1).T
     total = (packed[n_dp:] + other[n_dp:]).reshape(-1)
     gain_one_sum, gain_two_sum = total[:width], total[width : 2 * width]
-    tables = [x[-1, : heads * buckets].reshape(heads, buckets) for x in (low, high)]
+    tables = [x[-1].reshape(heads, 64)[:, :buckets] for x in (low, high)]
     table_sum = jnp.concatenate(tables, 0).T
     weights = jnp.sum(got_four[:, :w_rows].astype(F32), axis=0)
-    grad_qkv_shard = jnp.transpose(weights[: 3 * shard].reshape(3, shard, cols), (1, 0, 2))
-    grad_o_shard = weights[3 * shard :].reshape(wo_rows, width)
+    full = [jnp.concatenate([weights[8 * c : 8 * c + 8], weights[32 + 4 * c : 36 + 4 * c]], 0) for c in range(4)]
+    grad_qkv_shard = jnp.stack(full[:3], 1)
+    grad_o_shard = full[3].reshape(wo_rows, width)
     return (
         activations,
         input_grad,

time: 309 us -> 275 us (0.89)
  local copies, waits for them, and re-layouts: 105 us -> 54.3 us
  blocking collectives: 51.9 us -> 8.6 us
  matrix products: 52.6 us -> 76.9 us
  other arithmetic: 24.7 us -> 45.9 us
  Pallas kernels: 0 us -> 20.2 us
  waiting for transfers between devices: 39.6 us -> 23.3 us
  starting transfers between devices: 29 us -> 39.8 us
    all_to_all x1 -> x0, blocking collectives: 43 us -> none  [per_device(): got_three = lax.all_to_all(jnp.concatenate([both, r_send], 1), ALL, 0, 0)]
    dot_general x24 -> x32, matrix products: 39.8 us -> 73.8 us  [dot(): lax.dot_general(left, right, (dims, ((), ())), precision=precision, prefe...]
    concatenate x1, local copies, waits for them, and re-layouts: 26.8 us -> 0.11 us  [per_device(): jnp.concatenate([x[:8] for x in pieces] + [x[8:] for x in pieces], 0)]
    pallas_call x0 -> x2, Pallas kernels: none -> 20.2 us  [the longest x1 10.9 us: attend_back(): pl.pallas_call(attend_back_kernel, in_specs=[WHOLE] * 8 + [ANYWHERE] * 4,...]
    reshape x14 -> x1, local copies, waits for them, and re-layouts: 16.8 us -> 0.61 us  [per_device(): grad_o_shard = full[3].reshape(wo_rows, width)]
    all_to_all x1, waiting for transfers between devices: 25 us -> 9.19 us  [per_device(): got_four = lax.all_to_all(send_four, 'dp', 0, 0)]
    all_to_all x0 -> x1, waiting for transfers between devices: none -> 13.8 us  [per_device(): got_three = lax.all_to_all(jnp.concatenate([both, r_send], 1), ALL, 0, 0)]
    all_to_all x1, waiting for transfers between devices: 12 us -> 0.01 us  [per_device(): got_one = lax.all_to_all(send_one, 'dp', 0, 0)]
  transfers between devices with their start and end apart: 6 -> 7, of which waited for: 4 -> 3; matrix products, arithmetic and copies ran while one was open for 13% -> 41% of each run, Pallas kernels for 0% -> 0%
where the time goes in v2:
time: 275 us; the launch traced here: 271 us
  matrix products  76.9 us (28%)
  local copies, waits for them, and re-layouts  54.3 us (20%)
  other arithmetic  45.9 us (17%)
  starting transfers between devices  39.8 us (14%)
  waiting for transfers between devices  23.3 us (8%)
  Pallas kernels  20.2 us (7%)
  blocking collectives  8.6 us (3%)
    dot_general x32, matrix products, dot(): lax.dot_general(left, right, (dims, ((), ())), precision=precision, prefe...  73.8 us
    all_to_all x1, waiting for transfers between devices, per_device(): got_three = lax.all_to_all(jnp.concatenate([both, r_send], 1), ALL, 0, 0)  13.8 us
    all_to_all x1, starting transfers between devices, per_device(): got_one = lax.all_to_all(send_one, 'dp', 0, 0)  12.3 us
    pallas_call x1, Pallas kernels, attend_back(): pl.pallas_call(attend_back_kernel, in_specs=[WHOLE] * 8 + [ANYWHERE] * 4,...  10.9 us
    all_to_all x1, starting transfers between devices, per_device(): got_three = lax.all_to_all(jnp.concatenate([both, r_send], 1), ALL, 0, 0)  9.79 us
    all_to_all x1, starting transfers between devices, per_device(): lax.all_to_all(send_two.reshape(n_dp * n_t, cap, width), ALL, 0, 0)  9.43 us
    pallas_call x1, Pallas kernels, attend(): pl.pallas_call(attend_kernel, in_specs=[SCALAR] + [WHOLE] * 4, out_specs=...  9.31 us
    all_to_all x1, waiting for transfers between devices, per_device(): got_four = lax.all_to_all(send_four, 'dp', 0, 0)  9.19 us
  transfers between devices with their start and end apart: 7, of which 3 were waited for; matrix products, arithmetic and copies ran while one was open for 41% of the time, Pallas kernels for 0%

profile of v2, /device:TPU:1, one launch (start us, length us, event | category | flops | bytes accessed | tf_op | source)
XLA Modules:
  0.0 270.6 jit_solution(10524284426932507951)
XLA Ops:
  8.6 1.8 fusion.4
  10.4 12.3 %all-to-all-start = ((bf16[64,56,384]{2,1,0:T(8,128)(2,1)}), bf16[64,56,384]{2,1,0:T(8,128)(2,1)}, u32[]{:S(2)}, u32[]{:S(2)}) async-start(bf16[64,56,384]{2,1,0:T(8,128)(2,1)} %fusion.4), calls=%async_computation | async-start | bytes 5505024 | tf_op jit(solution)/shard_map/all_to_all | solution.py:236
  25.3 2.7 all_gather.9
  28.1 6.1 %fusion.170 = (bf16[5,768,1024]{1,2,0:T(8,128)(2,1)}, pred[5,768,1024]{1,2,0:T(32,128)(4,1)S(1)}) fusion(pred[5,768]{1,0:T(8,128)(4,1)S(1)} %broadcast_compare_fusion.1, s32[5,768]{1,0:T(8,128)S(1)} %broadcast_add_fusion), kind=kLoop, calls=%fused_computation.270 | loop fusion | flops 11796480 | bytes 11815680 | tf_op jit(solution)/shard_map/convert_element_type | solution.py:197
  34.3 2.0 fusion.65
  42.9 1.9 copy.90
  44.8 3.2 %slice.289 = f32[6,130816]{1,0:T(8,128)} slice(f32[6,131072]{1,0:T(8,128)S(1)} %bitcast.306), slice={[0:6], [255:131071]} | slice | bytes 6279168 | tf_op jit(solution)/shard_map/slice | solution.py:254
  47.9 6.4 %reshape.472 = f32[6,256,511]{2,1,0:T(8,128)} reshape(f32[6,130816]{1,0:T(8,128)} %slice.289) | data formatting | bytes 6279168 | tf_op jit(solution)/shard_map/reshape | solution.py:255
  54.4 2.8 %fusion.67 = bf16[5,1024,256]{2,1,0:T(8,128)(2,1)} fusion(bf16[5,1024,256]{2,1,0:T(8,128)(2,1)} %fusion.65, bf16[256,768]{1,0:T(8,128)(2,1)S(1)} %all_gather.9, pred[5,768,1024]{1,2,0:T(32,128)(4,1)} %copy-done.23), kind=kOutput, calls=%fused_computation.109 | convolution fusion | flops 402915328 | bytes 1703936 | tf_op jit(solution)/shard_map/dot_general | solution.py:21
  64.8 2.6 fusion.73
  67.4 2.8 %fusion.77 = bf16[5,256,1024]{2,1,0:T(8,128)(2,1)} fusion(bf16[5,256,1024]{2,1,0:T(8,128)(2,1)} %fusion.73, bf16[256,768]{1,0:T(8,128)(2,1)S(1)} %all_gather.9, pred[5,768,1024]{1,2,0:T(32,128)(4,1)} %copy-done.23), kind=kOutput, calls=%fused_computation.119 | convolution fusion | flops 402915328 | bytes 1703936 | tf_op jit(solution)/shard_map/dot_general | solution.py:21
  70.2 3.3 %fusion.81.x_ref = bf16[5,256,1024]{2,1,0:T(8,128)(2,1)} fusion(bf16[5,256,1024]{2,1,0:T(8,128)(2,1)} %fusion.77, bf16[256,768]{1,0:T(8,128)(2,1)S(1)} %all_gather.9, pred[5,768,1024]{1,2,0:T(32,128)(4,1)} %copy-done.23), kind=kOutput, calls=%fused_computation.123 | convolution fusion | flops 402915328 | bytes 1703936 | tf_op jit(solution)/shard_map/dot_general | solution.py:21
  73.5 2.2 fusion.29
  78.0 2.4 pad_maximum_fusion.s_any
  80.4 3.0 %fusion.1 = (pred[4,384,1024]{2,1,0:T(32,128)(4,1)}, bf16[4,384,1024]{2,1,0:T(8,128)(2,1)}) fusion(s32[4,384]{1,0:T(4,128)S(1)} %add_add_fusion, pred[4,384]{1,0:T(4,128)(4,1)S(1)} %broadcast_compare_fusion.2), kind=kLoop, calls=%fused_computation.3 | loop fusion | flops 4718592 | bytes 4726272 | tf_op jit(solution)/shard_map/and | solution.py:196
  83.4 9.3 %shard_map.240 = (f32[128,768]{1,0:T(8,128)S(1)}, bf16[128,768]{1,0:T(8,128)(2,1)}, bf16[256,384]{1,0:T(8,128)(2,1)S(1)}, bf16[3,256,384]{2,1,0:T(8,128)(2,1)S(1...) custom-call(s32[1]{0:T(128)} %bitcast.t_ref, bf16[64,56,384]{2,1,0:T(8,128)(2,1)} %all-to-all-done.got_ref.got_any, ...), custom_call_target="tpu_custom_call" | custom-call | flops 4000000000 | bytes 14000000 | tf_op jit(solution)/shard_map/pallas_call | solution.py:82
  100.8 2.4 fusion.82
  106.4 9.4 %all-to-all-start.1 = ((bf16[128,2,768]{2,1,0:T(2,128)(2,1)}), bf16[128,2,768]{2,1,0:T(2,128)(2,1)}, u32[]{:S(2)}, u32[]{:S(2)}) async-start(bf16[128,2,768]{2,1,0:T(2,128)(2,1)} %bitcast.18), calls=%async_computation.1 | async-start | bytes 786432 | tf_op jit(solution)/shard_map/all_to_all | solution.py:266
  115.9 3.1 %all_gather.10 = bf16[2,128,768]{2,1,0:T(8,128)(2,1)S(1)} all-gather(bf16[1,128,768]{2,1,0:T(8,128)(2,1)} %all_gather_reshape.3), channel_id=1, replica_groups=mesh['dp'=64,'tensor'=2] {'tensor'}, dimensions={0}, use_global_device_ids=true | all-gather | bytes 589824 | tf_op jit(solution)/shard_map/all_gather | solution.py:247
  120.2 2.1 copy.101
  122.3 2.6 reshape.486
  124.9 3.1 %fusion.173 = (bf16[64,16,384]{2,1,0:T(8,128)(2,1)}, bf16[64,16,384]{2,1,0:T(8,128)(2,1)}, bf16[64,16,384]{2,1,0:T(8,128)(2,1)}) fusion(bf16[64,56,384]{2,1,0:T(8,128)(2,1)} %all-to-all-done.got_ref.got_any), kind=kLoop, calls=%fused_computation.272 | loop fusion | bytes 4718592 | tf_op jit(solution)/shard_map/slice | solution.py:325
  134.7 5.2 %multiply_convert_fusion = (bf16[256,1536]{1,0:T(8,128)(2,1)S(1)}, f32[256,1536]{1,0:T(8,128)}, f32[256,1536]{1,0:T(8,128)}) fusion(bf16[256,768]{1,0:T(8,128)(2,1)S(1)} %reshape.474, bf16[1,768,1536]{2,1,0:T(8,128)(2,1)S(1)} %copy-done), kind=kOutput, calls=%fused_computation.51 | convolution fusion | flops 629538816 | bytes 6684672 | tf_op jit(solution)/shard_map/dot_general | solution.py:21
  145.5 1.9 convert_element_type.194
  149.9 3.8 %add_convert_fusion = bf16[256,1536]{1,0:T(8,128)(2,1)S(1)} fusion(f32[256,1536]{1,0:T(8,128)} %get-tuple-element.71, bf16[256,768]{1,0:T(8,128)(2,1)} %convert_element_type.194, bf16[1,1536,768]{2,1,0:T(8,128)(2,1)} %param.25, f32[256,1536]{1,0:T(8,128)} %get-tuple-element.109), kind=kOutput, calls=%fused_computation.50 | convolution fusion | flops 609484800 | bytes 6684672 | tf_op jit(solution)/shard_map/dot_general | solution.py:21
  156.3 1.9 reshape.476
  158.2 3.4 %fusion.26 = bf16[128,5,768]{2,1,0:T(8,128)(2,1)} fusion(bf16[128,1,384]{2,1,0:T(2,128)(2,1)} %reshape.491, bf16[128,2,768]{2,1,0:T(2,128)(2,1)} %reshape.476, bf16[128,2,768]{2,1,0:T(2,128)(2,1)S(1)} %copy-done.31), kind=kLoop, calls=%fused_computation.42 | loop fusion | flops 3932160 | bytes 1867776 | tf_op jit(solution)/shard_map/concatenate | solution.py:295
  161.6 9.8 %all-to-all-start.2 = ((bf16[128,5,768]{2,1,0:T(8,128)(2,1)}), bf16[128,5,768]{2,1,0:T(8,128)(2,1)}, u32[]{:S(2)}, u32[]{:S(2)}) async-start(bf16[128,5,768]{2,1,0:T(8,128)(2,1)} %fusion.26), calls=%async_computation.2 | async-start | bytes 3145728 | tf_op jit(solution)/shard_map/all_to_all | solution.py:295
  171.5 3.2 %pad_maximum_fusion.1.xot_any = bf16[4,1024,256]{2,1,0:T(8,128)(2,1)} fusion(bf16[1,1024,256]{2,1,0:T(8,128)(2,1)} %fusion.85, bf16[1,1024,256]{2,1,0:T(8,128)(2,1)} %fusion.84, bf16[1,1024,256]{2,1,0:T(8,128)(2,1)} %fusion.83, bf16[1,1024,256]{2,1,0:T(8,128)(2,1)} %fusion.82), kind=kLoop, calls=%fused_computation.28 | loop fusion | flops 3145728 | bytes 4194304 | tf_op jit(solution)/shard_map/stack | solution.py:316
  175.9 3.0 %convolution_bitcast_fusion.1 = f32[1,768,1536]{2,1,0:T(8,128)} fusion(bf16[256,768]{1,0:T(8,128)(2,1)S(1)} %copy-done.13, bf16[256,1536]{1,0:T(8,128)(2,1)S(1)} %copy-done.37), kind=kOutput, calls=%fused_computation.9 | convolution fusion | flops 603979776 | bytes 5898240 | tf_op jit(solution)/shard_map/dot_general | solution.py:21
  178.9 3.1 %convolution_bitcast_fusion = f32[1,1536,768]{2,1,0:T(8,128)} fusion(bf16[256,1536]{1,0:T(8,128)(2,1)S(1)} %copy-done.19, f32[256,768]{1,0:T(8,128)S(1)} %copy-done.17, f32[256]{0:T(256)S(1)} %copy-done.45), kind=kOutput, calls=%fused_computation.8 | convolution fusion | flops 604372992 | bytes 6292480 | tf_op jit(solution)/shard_map/dot_general | solution.py:21
  182.0 13.8 %all-to-all-done.2 = bf16[128,5,768]{2,1,0:T(8,128)(2,1)} async-done(((bf16[128,5,768]{2,1,0:T(8,128)(2,1)}), bf16[128,5,768]{2,1,0:T(8,128)(2,1)}, u32[]{:S(2)}, u32[]{:S(2)}) %all-to-all-start.2) | async-done | bytes 983072 | tf_op jit(solution)/shard_map/all_to_all | solution.py:295
  195.8 2.0 convert_reduce_fusion.1
  199.1 2.0 reshape.481
  202.8 1.9 fusion.171
  204.8 2.9 %all_gather.11.ga_ref = bf16[256,768]{1,0:T(8,128)(2,1)S(1)} all-gather(bf16[128,768]{1,0:T(8,128)(2,1)S(1)} %get-tuple-element.68), channel_id=1, replica_groups=mesh['dp'=64,'tensor'=2] {'tensor'}, dimensions={0}, use_global_device_ids=true | all-gather | bytes 589824 | tf_op jit(solution)/shard_map/all_gather | solution.py:313
  207.6 10.9 %shard_map.241 = (bf16[64,56,384]{2,1,0:T(8,128)(2,1)}, bf16[3,256,384]{2,1,0:T(8,128)(2,1)S(1)}) custom-call(bf16[256,768]{1,0:T(8,128)(2,1)S(1)} %all_gather.11.ga_ref, bf16[384,768]{1,0:T(8,128)(2,1)S(1)} %copy-done.6, bf16[3,256,384]{2,1,0:T(8,128)(2,1)S(1)} %copy-done.4, bf16[6,256,256]{2,1,0:T(8,128)(2,1)S(1)} %copy-done.2, ...), custom_call_target="tpu_custom_call" | custom-call | flops 4000000000 | bytes 16000000 | tf_op jit(solution)/shard_map/pallas_call | solution.py:173
  219.4 6.0 %all-to-all-start.3 = ((bf16[64,56,384]{2,1,0:T(8,128)(2,1)}), bf16[64,56,384]{2,1,0:T(8,128)(2,1)}, u32[]{:S(2)}, u32[]{:S(2)}) async-start(bf16[64,56,384]{2,1,0:T(8,128)(2,1)} %get-tuple-element.25), calls=%async_computation.3 | async-start | bytes 5505024 | tf_op jit(solution)/shard_map/all_to_all | solution.py:323
  225.3 2.0 reshape.480
  227.3 3.1 %fusion.61 = f32[256,768]{1,0:T(8,128)} fusion(bf16[1024,384]{1,0:T(8,128)(2,1)} %bitcast.316, pred[5,768,1024]{1,2,0:T(32,128)(4,1)} %copy-done.23, bf16[3,256,384]{2,1,0:T(8,128)(2,1)S(1)} %copy-done.8), kind=kOutput, calls=%fused_computation.103 | convolution fusion | flops 604241920 | bytes 2555904 | tf_op jit(solution)/shard_map/dot_general | solution.py:21
  230.4 3.1 %fusion.16 = f32[256,768]{1,0:T(8,128)} fusion(pred[5,768,1024]{1,2,0:T(32,128)(4,1)} %copy-done.23, bf16[1024,384]{1,0:T(8,128)(2,1)} %bitcast.311, bf16[3,256,384]{2,1,0:T(8,128)(2,1)S(1)} %copy-done.8), kind=kOutput, calls=%fused_computation.32 | convolution fusion | flops 604241920 | bytes 2555904 | tf_op jit(solution)/shard_map/dot_general | solution.py:21
  233.5 3.1 %fusion.60 = f32[256,768]{1,0:T(8,128)} fusion(bf16[1024,384]{1,0:T(8,128)(2,1)} %bitcast.314, pred[5,768,1024]{1,2,0:T(32,128)(4,1)} %copy-done.23, bf16[3,256,384]{2,1,0:T(8,128)(2,1)S(1)} %copy-done.8), kind=kOutput, calls=%fused_computation.102 | convolution fusion | flops 604241920 | bytes 2555904 | tf_op jit(solution)/shard_map/dot_general | solution.py:21
  236.6 3.4 %fusion.51 = f32[256,768]{1,0:T(8,128)} fusion(f32[256,768]{1,0:T(8,128)} %fusion.16, pred[5,768,1024]{1,2,0:T(32,128)(4,1)} %copy-done.23, bf16[1024,384]{1,0:T(8,128)(2,1)} %bitcast.312, bf16[3,256,384]{2,1,0:T(8,128)(2,1)S(1)} %copy-done.8), kind=kOutput, calls=%fused_computation.97 | convolution fusion | flops 604438528 | bytes 3342336 | tf_op jit(solution)/shard_map/dot_general | solution.py:21
  240.0 3.6 %fusion.53 = f32[256,768]{1,0:T(8,128)} fusion(f32[256,768]{1,0:T(8,128)} %fusion.61, f32[256,768]{1,0:T(8,128)} %fusion.60, pred[5,768,1024]{1,2,0:T(32,128)(4,1)} %copy-done.23, bf16[1024,384]{1,0:T(8,128)(2,1)} %bitcast.315, bf16[3,256,384]{2,1,0:T(8,128)(2,1)S(1)} %copy-done.8), kind=kOutput, calls=%fused_computation.99 | convolution fusion | flops 604635136 | bytes 4128768 | tf_op jit(solution)/shard_map/dot_general | solution.py:21
  243.7 3.7 %fusion.50 = f32[256,768]{1,0:T(8,128)} fusion(f32[256,768]{1,0:T(8,128)} %fusion.53, f32[256,768]{1,0:T(8,128)} %fusion.51, pred[5,768,1024]{1,2,0:T(32,128)(4,1)} %copy-done.23, bf16[1024,384]{1,0:T(8,128)(2,1)} %bitcast.313, bf16[3,256,384]{2,1,0:T(8,128)(2,1)S(1)} %copy-done.8), kind=kOutput, calls=%fused_computation.96 | convolution fusion | flops 604635136 | bytes 4128768 | tf_op jit(solution)/shard_map/dot_general | solution.py:21
  248.9 2.0 fusion.87
  252.0 9.2 %all-to-all-done.3 = bf16[64,56,384]{2,1,0:T(8,128)(2,1)} async-done(((bf16[64,56,384]{2,1,0:T(8,128)(2,1)}), bf16[64,56,384]{2,1,0:T(8,128)(2,1)}, u32[]{:S(2)}, u32[]{:S(2)}) %all-to-all-start.3) | async-done | bytes 2752544 | tf_op jit(solution)/shard_map/all_to_all | solution.py:323
  262.5 2.0 convert_reduce_fusion
  (248 shorter events, 71.5 us)
Async XLA Ops:
  0.6 134.1 %copy-start = (bf16[1,768,1536]{2,1,0:T(8,128)(2,1)S(1)}, bf16[1,768,1536]{2,1,0:T(8,128)(2,1)}, u32[]{:S(2)}) copy-start(bf16[1,768,1536]{2,1,0:T(8,128)(2,1)} %param.24) | copy-start | bytes 7077892
  10.4 14.1 %copy-start.20 = (bf16[128,768]{1,0:T(8,128)(2,1)S(1)}, bf16[128,768]{1,0:T(8,128)(2,1)}, u32[]{:S(2)}) copy-start(bf16[128,768]{1,0:T(8,128)(2,1)} %param.17) | copy-start | bytes 589828
  10.4 14.8 %copy-start.41 = (f32[768]{0:T(1024)S(1)}, f32[768]{0:T(1024)}, u32[]{:S(2)}) copy-start(f32[768]{0:T(1024)} %param.18) | copy-start | bytes 9220
  10.4 17.6 %copy-start.60 = (pred[5]{0:T(512)(128)(4,1)S(1)}, pred[5]{0:T(512)(128)(4,1)}, u32[]{:S(2)}) copy-start(pred[5]{0:T(512)(128)(4,1)} %constant.163.clone) | copy-start | bytes 19
  10.4 17.7 %copy-start.59 = (s32[5]{0:T(128)S(1)}, s32[5]{0:T(128)}, u32[]{:S(2)}) copy-start(s32[5]{0:T(128)} %constant.162.clone) | copy-start | bytes 64
  10.4 73.0 %all-to-all-start = ((bf16[64,56,384]{2,1,0:T(8,128)(2,1)}), bf16[64,56,384]{2,1,0:T(8,128)(2,1)}, u32[]{:S(2)}, u32[]{:S(2)}) async-start(bf16[64,56,384]{2,1,0:T(8,128)(2,1)} %fusion.4), calls=%async_computation | async-start | bytes 5505024 | tf_op jit(solution)/shard_map/all_to_all | solution.py:236
  25.2 9.1 %copy-start.55 = (f32[128]{0:T(128)}, f32[128]{0:T(128)S(1)}, u32[]{:S(2)}) copy-start(f32[128]{0:T(128)S(1)} %get-tuple-element.106) | copy-start | bytes 1540
  67.4 10.3 %slice-start = ((s8[7864320]{0:T(1024)(128)(4,1)}), s8[4194304]{0:T(1024)(128)(4,1)S(1)}, s32[]{:S(2)}) async-start(s8[7864320]{0:T(1024)(128)(4,1)} %bitcast.304), calls=%async_computation.4 | async-start | bytes 8388608
  70.2 7.5 %slice-start.1 = ((s8[7864320]{0:T(1024)(128)(4,1)}), s8[3670016]{0:T(1024)(128)(4,1)S(1)}, s32[]{:S(2)}) async-start(s8[7864320]{0:T(1024)(128)(4,1)} %bitcast.304), calls=%async_computation.5 | async-start | bytes 7340032
  83.4 9.3 %copy-start.32 = (pred[4,384,1024]{2,1,0:T(32,128)(4,1)S(1)}, pred[4,384,1024]{2,1,0:T(32,128)(4,1)}, u32[]{:S(2)}) copy-start(pred[4,384,1024]{2,1,0:T(32,128)(4,1)} %get-tuple-element.103) | copy-start | bytes 4718596
  92.8 3.3 %copy-start.9 = (bf16[256,384]{1,0:T(8,128)(2,1)}, bf16[256,384]{1,0:T(8,128)(2,1)S(1)}, u32[]{:S(2)}) copy-start(bf16[256,384]{1,0:T(8,128)(2,1)S(1)} %get-tuple-element.23) | copy-start | bytes 589828
  95.6 7.7 %collective-permute-start = (bf16[128,768]{1,0:T(8,128)(2,1)}, bf16[128,768]{1,0:T(8,128)(2,1)}, u32[]{:S(2)}, u32[]{:S(2)}) collective-permute-start(bf16[128,768]{1,0:T(8,128)(2,1)} %get-tuple-element.19), channel_id=1, source_target_pairs={{0,1},{1,0},{2,3},{3,2},{4,5},{5,4},{6,7},{7,6},{8,9},{9,8},{10,11... | collective-permute-start | bytes 589832 | tf_op jit(solution)/shard_map/ppermute | solution.py:17
  100.8 4.3 %copy-start.40 = (f32[768]{0:T(1024)S(1)}, f32[768]{0:T(1024)}, u32[]{:S(2)}) copy-start(f32[768]{0:T(1024)} %param.22) | copy-start | bytes 9220
  100.8 4.3 %copy-start.49 = (s32[128]{0:T(128)S(1)}, s32[128]{0:T(128)}, u32[]{:S(2)}) copy-start(s32[128]{0:T(128)} %copy-done.48) | copy-start | bytes 1540
  104.9 15.3 %copy-start.46 = (f32[128]{0:T(128)}, f32[128]{0:T(128)S(1)}, u32[]{:S(2)}) copy-start(f32[128]{0:T(128)S(1)} %get-tuple-element.108) | copy-start | bytes 1540
  106.4 21.6 %all-to-all-start.1 = ((bf16[128,2,768]{2,1,0:T(2,128)(2,1)}), bf16[128,2,768]{2,1,0:T(2,128)(2,1)}, u32[]{:S(2)}, u32[]{:S(2)}) async-start(bf16[128,2,768]{2,1,0:T(2,128)(2,1)} %bitcast.18), calls=%async_computation.1 | async-start | bytes 786432 | tf_op jit(solution)/shard_map/all_to_all | solution.py:266
  129.2 12.3 %copy-start.12 = (bf16[256,768]{1,0:T(8,128)(2,1)}, bf16[256,768]{1,0:T(8,128)(2,1)S(1)}, u32[]{:S(2)}) copy-start(bf16[256,768]{1,0:T(8,128)(2,1)S(1)} %reshape.474) | copy-start | bytes 1179652
  134.7 5.2 %copy-start.16 = (f32[256,768]{1,0:T(8,128)S(1)}, f32[256,768]{1,0:T(8,128)}, u32[]{:S(2)}) copy-start(f32[256,768]{1,0:T(8,128)} %reshape.486) | copy-start | bytes 2359300
  134.7 5.2 %copy-start.25 = (bf16[1,1536,768]{2,1,0:T(8,128)(2,1)S(1)}, bf16[1,1536,768]{2,1,0:T(8,128)(2,1)}, u32[]{:S(2)}) copy-start(bf16[1,1536,768]{2,1,0:T(8,128)(2,1)} %param.25) | copy-start | bytes 7077892
  141.5 2.9 %copy-start.15 = (f32[2,64,2,768]{3,2,1,0:T(2,128)S(1)}, f32[2,64,2,768]{3,2,1,0:T(2,128)}, u32[]{:S(2)}) copy-start(f32[2,64,2,768]{3,2,1,0:T(2,128)} %reshape.489) | copy-start | bytes 2359300
  141.5 2.9 %copy-start.39 = (f32[64,2,2]{2,1,0:T(2,128)S(1)}, f32[64,2,2]{2,1,0:T(2,128)}, u32[]{:S(2)}) copy-start(f32[64,2,2]{2,1,0:T(2,128)} %mul.311) | copy-start | bytes 3076
  142.6 4.8 %copy-start.30 = (bf16[256,768]{1,0:T(8,128)(2,1)S(1)}, bf16[256,768]{1,0:T(8,128)(2,1)}, u32[]{:S(2)}) copy-start(bf16[256,768]{1,0:T(8,128)(2,1)} %get-tuple-element.81) | copy-start | bytes 1179652
  149.9 4.7 %copy-start.35 = (f32[256,768]{1,0:T(8,128)S(1)}, f32[256,768]{1,0:T(8,128)}, u32[]{:S(2)}) copy-start(f32[256,768]{1,0:T(8,128)} %fusion.135) | copy-start | bytes 2359300
  154.7 3.5 %copy-start.31 = (bf16[128,2,768]{2,1,0:T(2,128)(2,1)S(1)}, bf16[128,2,768]{2,1,0:T(2,128)(2,1)}, u32[]{:S(2)}) copy-start(bf16[128,2,768]{2,1,0:T(2,128)(2,1)} %reshape.475) | copy-start | bytes 1179652
  161.6 34.2 %all-to-all-start.2 = ((bf16[128,5,768]{2,1,0:T(8,128)(2,1)}), bf16[128,5,768]{2,1,0:T(8,128)(2,1)}, u32[]{:S(2)}, u32[]{:S(2)}) async-start(bf16[128,5,768]{2,1,0:T(8,128)(2,1)} %fusion.26), calls=%async_computation.2 | async-start | bytes 3145728 | tf_op jit(solution)/shard_map/all_to_all | solution.py:295
  171.4 3.3 %copy-start.11 = (f32[128,768]{1,0:T(8,128)S(1)}, f32[128,768]{1,0:T(8,128)}, u32[]{:S(2)}) copy-start(f32[128,768]{1,0:T(8,128)} %copy-done.10) | copy-start | bytes 1179652
  171.4 3.3 %copy-start.27 = (f32[768,64]{0,1:T(8,128)S(1)}, f32[768,64]{0,1:T(8,128)}, u32[]{:S(2)}) copy-start(f32[768,64]{0,1:T(8,128)} %param.23) | copy-start | bytes 589828
  171.4 3.3 %copy-start.47 = (f32[128]{0:T(128)S(1)}, f32[128]{0:T(128)}, u32[]{:S(2)}) copy-start(f32[128]{0:T(128)} %copy-done.46) | copy-start | bytes 1540
  171.4 3.9 %copy-start.52 = (s32[128,1]{0,1:T(1,128)S(1)}, s32[128,1]{0,1:T(1,128)}, u32[]{:S(2)}) copy-start(s32[128,1]{0,1:T(1,128)} %param.28) | copy-start | bytes 1540
  171.4 4.5 %copy-start.13 = (bf16[256,768]{1,0:T(8,128)(2,1)S(1)}, bf16[256,768]{1,0:T(8,128)(2,1)}, u32[]{:S(2)}) copy-start(bf16[256,768]{1,0:T(8,128)(2,1)} %copy-done.12) | copy-start | bytes 1179652
  171.5 4.5 %copy-start.37 = (bf16[256,1536]{1,0:T(8,128)(2,1)S(1)}, bf16[256,1536]{1,0:T(8,128)(2,1)}, u32[]{:S(2)}) copy-start(bf16[256,1536]{1,0:T(8,128)(2,1)} %copy-done.36) | copy-start | bytes 2359300
  175.9 3.0 %copy-start.17 = (f32[256,768]{1,0:T(8,128)S(1)}, f32[256,768]{1,0:T(8,128)}, u32[]{:S(2)}) copy-start(f32[256,768]{1,0:T(8,128)} %reshape.486) | copy-start | bytes 2359300
  175.9 3.0 %copy-start.19 = (bf16[256,1536]{1,0:T(8,128)(2,1)S(1)}, bf16[256,1536]{1,0:T(8,128)(2,1)}, u32[]{:S(2)}) copy-start(bf16[256,1536]{1,0:T(8,128)(2,1)} %copy-done.18) | copy-start | bytes 2359300
  175.9 3.0 %copy-start.45 = (f32[256]{0:T(256)S(1)}, f32[256]{0:T(256)}, u32[]{:S(2)}) copy-start(f32[256]{0:T(256)} %multiply_reduce_fusion.4) | copy-start | bytes 3076
  201.2 6.5 %copy-start.2 = (bf16[6,256,256]{2,1,0:T(8,128)(2,1)S(1)}, bf16[6,256,256]{2,1,0:T(8,128)(2,1)}, u32[]{:S(2)}) copy-start(bf16[6,256,256]{2,1,0:T(8,128)(2,1)} %copy-done.1) | copy-start | bytes 2359300
  201.2 6.5 %copy-start.4 = (bf16[3,256,384]{2,1,0:T(8,128)(2,1)S(1)}, bf16[3,256,384]{2,1,0:T(8,128)(2,1)}, u32[]{:S(2)}) copy-start(bf16[3,256,384]{2,1,0:T(8,128)(2,1)} %copy-done.3) | copy-start | bytes 1769476
  201.2 6.5 %copy-start.6 = (bf16[384,768]{1,0:T(8,128)(2,1)S(1)}, bf16[384,768]{1,0:T(8,128)(2,1)}, u32[]{:S(2)}) copy-start(bf16[384,768]{1,0:T(8,128)(2,1)} %copy-done.5) | copy-start | bytes 1769476
  219.4 8.0 %copy-start.8 = (bf16[3,256,384]{2,1,0:T(8,128)(2,1)S(1)}, bf16[3,256,384]{2,1,0:T(8,128)(2,1)}, u32[]{:S(2)}) copy-start(bf16[3,256,384]{2,1,0:T(8,128)(2,1)} %copy-done.7) | copy-start | bytes 1769476
  219.4 41.8 %all-to-all-start.3 = ((bf16[64,56,384]{2,1,0:T(8,128)(2,1)}), bf16[64,56,384]{2,1,0:T(8,128)(2,1)}, u32[]{:S(2)}, u32[]{:S(2)}) async-start(bf16[64,56,384]{2,1,0:T(8,128)(2,1)} %get-tuple-element.25), calls=%async_computation.3 | async-start | bytes 5505024 | tf_op jit(solution)/shard_map/all_to_all | solution.py:323
  243.6 5.3 %copy-start.50 = (s32[128]{0:T(128)S(1)}, s32[128]{0:T(128)}, u32[]{:S(2)}) copy-start(s32[128]{0:T(128)} %copy-done.48) | copy-start | bytes 1540
  243.6 5.3 %copy-start.57 = (f32[128]{0:T(128)S(1)}, f32[128]{0:T(128)}, u32[]{:S(2)}) copy-start(f32[128]{0:T(128)} %select_reduce_fusion) | copy-start | bytes 1540
  243.6 7.3 %copy-start.22 = (bf16[128,768]{1,0:T(8,128)(2,1)S(1)}, bf16[128,768]{1,0:T(8,128)(2,1)}, u32[]{:S(2)}) copy-start(bf16[128,768]{1,0:T(8,128)(2,1)} %param.17) | copy-start | bytes 589828
  247.3 3.6 %copy-start.34 = (f32[256,768]{1,0:T(8,128)S(1)}, f32[256,768]{1,0:T(8,128)}, u32[]{:S(2)}) copy-start(f32[256,768]{1,0:T(8,128)} %fusion.50) | copy-start | bytes 2359300
  247.3 3.8 %copy-start.33 = (f32[128,768]{1,0:T(8,128)S(1)}, f32[128,768]{1,0:T(8,128)}, u32[]{:S(2)}) copy-start(f32[128,768]{1,0:T(8,128)} %get-tuple-element.69) | copy-start | bytes 1179652
  247.3 3.8 %copy-start.56 = (f32[128]{0:T(128)S(1)}, f32[128]{0:T(128)}, u32[]{:S(2)}) copy-start(f32[128]{0:T(128)} %copy-done.55) | copy-start | bytes 1540
  247.3 3.8 %copy-start.58 = (f32[128]{0:T(128)S(1)}, f32[128]{0:T(128)}, u32[]{:S(2)}) copy-start(f32[128]{0:T(128)} %get-tuple-element.105) | copy-start | bytes 1540
  248.4 2.5 collective-permute-start.1
  265.2 2.3 collective-permute-start.2
  (22 other events, 40.7 us)
